TPU v7x, 32 devices: a whole 2x2x4 slice. The times are simulated.
32 devices in a mesh: seq: 4 (over y, x), dp: 8 (over z, core).
Axes of the slice: x: 2, y: 2, z: 4, core: 2. Of those that a mesh axis runs over, the one named last changes fastest.
Arguments:
- tokens: bfloat16 [16, 512, 768], P('dp', 'seq'), may hold values from -6 to 6
- doc_starts: int32 [16, 8], P('dp'), may hold values from 0 to 511, as said below
- decay: float32 [2, 768], replicated, may hold values from -9 to -3.2
- first: float32 [2, 768], replicated, may hold values from -1 to 1
- mix: float32 [2, 5, 768], replicated, may hold values from 0 to 1
- ln_gain: float32 [2, 2, 768], replicated, may hold values from 0.5 to 1.5
- ln_bias: float32 [2, 2, 768], replicated, may hold values from -2 to 2
- att_kvr: bfloat16 [2, 768, 2304], P(None, 'dp'), may hold values from -0.21875 to 0.21875
- att_out: bfloat16 [2, 768, 768], P(None, 'dp'), may hold values from -1.75 to 1.75
- ffn_key: bfloat16 [2, 768, 3072], P(None, 'dp'), may hold values from -0.21875 to 0.21875
- ffn_recept: bfloat16 [2, 768, 768], P(None, 'dp'), may hold values from -0.21875 to 0.21875
- ffn_value: bfloat16 [2, 3072, 768], P(None, 'dp'), may hold values from -0.109375 to 0.109375
- cotangent: bfloat16 [16, 512, 768], P('dp', 'seq'), may hold values from -6 to 6
Outputs:
- output: bfloat16 [16, 512, 768], P('dp', 'seq')
- grad_tokens: bfloat16 [16, 512, 768], P('dp', 'seq')
- grad_decay: float32 [2, 768], P(None, 'dp')
- grad_first: float32 [2, 768], P(None, 'dp')
- grad_mix: float32 [2, 5, 768], P(None, None, 'dp')
- grad_gain: float32 [2, 2, 768], P(None, None, 'dp')
- grad_bias: float32 [2, 2, 768], P(None, None, 'dp')
- grad_kvr: float32 [2, 768, 2304], P(None, 'dp')
- grad_att_out: float32 [2, 768, 768], P(None, 'dp')
- grad_ffn_key: float32 [2, 768, 3072], P(None, 'dp')
- grad_ffn_recept: float32 [2, 768, 768], P(None, 'dp')
- grad_ffn_value: float32 [2, 3072, 768], P(None, 'dp')
Inputs may be any that keep to these rules, and one draw needn't show every extreme that they name: `doc_starts`: column 0 of every row is 0 and entries may repeat; in each aligned block of 2 rows at least one row lists only 0, so that its single document covers the whole row.
All inputs are finite; a program needn't handle non-finite values.
Results may differ from a plain program's by a relative error of at most 0.015.
Values may be sent and summed in bfloat16 or wider, within the bound.
A program may use at most 256 MiB of HBM per device.

v0:
```python
import math

import jax
import jax.numpy as jnp
from jax import lax
from jax.sharding import PartitionSpec as P

EPSILON = 1e-05


def from_behind(block, axis, distance):
    devices = range(lax.axis_size(axis))
    route = [(i - distance, i) for i in devices if i - distance in devices]
    return lax.ppermute(block, axis, route)


def normalize(stream, gain_row, bias_row):
    center = stream - jnp.mean(stream, -1, keepdims=True)
    spread = jnp.mean(center * center, -1, keepdims=True)
    return center * lax.rsqrt(spread + EPSILON) * gain_row + bias_row


def blend(hidden, edge_row, rates, starts):
    earlier = (
        jnp.concatenate([edge_row[:, None, :], hidden[:, :-1, :]], axis=1)
        * (1.0 - starts)[:, :, None]
    )
    return tuple((hidden * rates[j] + earlier * (1.0 - rates[j]) for j in range(rates.shape[0])))


def product(inputs, matrix):
    return jnp.einsum("rcd,de->rce", inputs, matrix, preferred_element_type=jnp.float32)


def product_back(grads, matrix):
    return jnp.einsum("rce,de->rcd", grads, matrix, preferred_element_type=jnp.float32)


def outer_sum(inputs, grads):
    return jnp.einsum("rcd,rce->de", inputs, grads, preferred_element_type=jnp.float32)


def wkv_tokens(key_proj, value_proj, decay_row, foremost_line_entry, numer_in, denom_in, starts):
    rows, length, width = key_proj.shape
    block = math.gcd(length, 64)
    count = length // block
    rate = jnp.exp(decay_row)
    local = jnp.arange(block, dtype=jnp.float32)
    lower = (local[:, None] > local[None, :]).astype(jnp.float32)
    grow = jnp.exp(local[:, None] * rate[None, :])
    shrink = jnp.exp(-(local[:, None] - 1.0) * rate[None, :])
    fade = jnp.exp(-local[:, None] * rate[None, :])
    keep_rate = jnp.exp(-rate)

    def one_block(carry, inputs):
        accrued_dividend_total, accrued_divisor_total = carry
        present_lookup_entry, present_payload_entry, start_now = inputs
        counted = jnp.cumsum(start_now, axis=1)
        same = lower[None] * (counted[:, :, None] == counted[:, None, :]).astype(jnp.float32)
        alive = (counted == 0.0).astype(jnp.float32)[:, :, None]
        key_exp = jnp.exp(present_lookup_entry)
        lifted = grow[None] * key_exp
        numer_sum = jnp.einsum(
            "rji,ric->rjc", same, lifted * present_payload_entry, precision=lax.Precision.HIGHEST
        )
        denom_sum = jnp.einsum("rji,ric->rjc", same, lifted, precision=lax.Precision.HIGHEST)
        present_dividend_term = (
            shrink[None] * numer_sum + fade[None] * alive * accrued_dividend_total[:, None, :]
        )
        present_divisor_term = (
            shrink[None] * denom_sum + fade[None] * alive * accrued_divisor_total[:, None, :]
        )
        present_reward_term = jnp.exp(foremost_line_entry + present_lookup_entry)
        recurrence_result = (
            present_dividend_term + present_reward_term * present_payload_entry
        ) / (present_divisor_term + present_reward_term)
        numer_end = (
            keep_rate * present_dividend_term[:, -1] + key_exp[:, -1] * present_payload_entry[:, -1]
        )
        denom_end = keep_rate * present_divisor_term[:, -1] + key_exp[:, -1]
        return ((numer_end, denom_end), recurrence_result)

    def split(values):
        return jnp.swapaxes(values.reshape((rows, count, block) + values.shape[2:]), 0, 1)

    carry_end, results = lax.scan(
        one_block, (numer_in, denom_in), (split(key_proj), split(value_proj), split(starts))
    )
    return jnp.swapaxes(results, 0, 1).reshape(rows, length, width)


def span_transform(key_proj, value_proj, decay_row, starts):
    length = key_proj.shape[1]
    rate = jnp.exp(decay_row)
    steps = jnp.arange(length, dtype=jnp.float32)
    last_start = jnp.max(steps[None, :] * starts, axis=1)
    after = (steps[None, :] >= last_start[:, None]).astype(jnp.float32)
    weight = jnp.exp(key_proj - (length - 1.0 - steps)[None, :, None] * rate) * after[:, :, None]
    carry_numer = jnp.sum(weight * value_proj, axis=1)
    carry_denom = jnp.sum(weight, axis=1)
    through = jnp.prod(1.0 - starts, axis=1)[:, None] * jnp.exp(-length * rate)[None, :]
    return (through, carry_numer, carry_denom)


def body(
    tokens,
    doc_starts,
    decay,
    first,
    mix,
    ln_gain,
    ln_bias,
    att_kvr,
    att_out,
    ffn_key,
    ffn_recept,
    ffn_value,
    cotangent,
):
    row_total, token_total, width = tokens.shape
    layer_total = decay.shape[0]
    batches = 2
    per_batch = row_total // batches
    positions = lax.axis_index("seq") * token_total + jnp.arange(token_total, dtype=jnp.int32)
    starts_all = jnp.any(doc_starts[:, :, None] == positions[None, None, :], axis=1).astype(
        jnp.float32
    )
    empty = jnp.zeros((per_batch, width), jnp.float32)

    def edge_of(hidden):
        return from_behind(hidden[:, -1, :], "seq", 1)

    def edge_back(grad_edge):
        return from_behind(grad_edge, "seq", -1)

    def chain_forward(through, carry_numer, carry_denom):
        incoming = (empty, empty)
        sent_numer, sent_denom = (carry_numer, carry_denom)
        for relay_turn in range(lax.axis_size("seq") - 1):
            incoming = from_behind((sent_numer, sent_denom), "seq", 1)
            sent_numer = through * incoming[0] + carry_numer
            sent_denom = through * incoming[1] + carry_denom
        return incoming

    def forward_layer(stream, level, matrices, starts):
        w_kvr, w_out, w_fkey, w_frec, w_fval = matrices
        hidden, norm_one = jax.vjp(normalize, stream, ln_gain[level, 0], ln_bias[level, 0])
        edge_row = edge_of(hidden)
        blends, blend_one = jax.vjp(
            lambda h_in, e_in, r_in: blend(h_in, e_in, r_in, starts),
            hidden,
            edge_row,
            mix[level, :3],
        )
        xk_low, xv_low, xr_low = [b.astype(jnp.bfloat16) for b in blends]
        key_proj = product(xk_low, w_kvr[:, :width])
        value_proj = product(xv_low, w_kvr[:, width : 2 * width])
        logit = product(xr_low, w_kvr[:, 2 * width :])
        transform, transform_one = jax.vjp(
            lambda k_in, v_in, d_in: span_transform(k_in, v_in, d_in, starts),
            key_proj,
            value_proj,
            decay[level],
        )
        numer_in, denom_in = chain_forward(transform[0], transform[1], transform[2])
        mixed, tokens_one = jax.vjp(
            lambda k_in, v_in, d_in, f_in, n_in, z_in: wkv_tokens(
                k_in, v_in, d_in, f_in, n_in, z_in, starts
            ),
            key_proj,
            value_proj,
            decay[level],
            first[level],
            numer_in,
            denom_in,
        )
        gated, gate_one = jax.vjp(lambda g_in, m_in: jax.nn.sigmoid(g_in) * m_in, logit, mixed)
        gated_low = gated.astype(jnp.bfloat16)
        middle = stream + product(gated_low, w_out)
        hidden_two, norm_two = jax.vjp(normalize, middle, ln_gain[level, 1], ln_bias[level, 1])
        edge_two = edge_of(hidden_two)
        blends_two, blend_two = jax.vjp(
            lambda h_in, e_in, r_in: blend(h_in, e_in, r_in, starts),
            hidden_two,
            edge_two,
            mix[level, 3:],
        )
        xk2_low, xr2_low = [b.astype(jnp.bfloat16) for b in blends_two]
        key_two = product(xk2_low, w_fkey)
        squared, square_one = jax.vjp(lambda k_in: jnp.square(jax.nn.relu(k_in)), key_two)
        squared_low = squared.astype(jnp.bfloat16)
        value_two = product(squared_low, w_fval)
        recept = product(xr2_low, w_frec)
        branch, branch_one = jax.vjp(
            lambda r_in, v_in: jax.nn.sigmoid(r_in) * v_in, recept, value_two
        )
        record = (
            norm_one,
            blend_one,
            xk_low,
            xv_low,
            xr_low,
            transform[0],
            numer_in,
            denom_in,
            transform_one,
            tokens_one,
            gate_one,
            gated_low,
            norm_two,
            blend_two,
            xk2_low,
            xr2_low,
            square_one,
            squared_low,
            branch_one,
        )
        return (middle + branch, record)

    gathered = []
    for level in range(layer_total):
        gathered.append(
            (
                lax.all_gather(att_kvr[level], "dp", axis=0, tiled=True),
                lax.all_gather(att_out[level], "dp", axis=0, tiled=True),
                lax.all_gather(ffn_key[level], "dp", axis=0, tiled=True),
                lax.all_gather(ffn_recept[level], "dp", axis=0, tiled=True),
                lax.all_gather(ffn_value[level], "dp", axis=0, tiled=True),
            )
        )
    pair_lists = [[] for level in range(layer_total)]
    vector_sums = [None] * layer_total
    outputs = []
    grad_parts = []
    for batch in range(batches):
        low_row = batch * per_batch
        starts = starts_all[low_row : low_row + per_batch]
        stream = tokens[low_row : low_row + per_batch].astype(jnp.float32)
        records = []
        for level in range(layer_total):
            stream, record = forward_layer(stream, level, gathered[level], starts)
            records.append(record)
        outputs.append(stream.astype(jnp.bfloat16))
        gradient = cotangent[low_row : low_row + per_batch].astype(jnp.float32)
        for level in reversed(range(layer_total)):
            backward_w_kvr, backward_w_out, backward_w_fkey, backward_w_frec, backward_w_fval = (
                gathered[level]
            )
            (
                backward_norm_one,
                backward_blend_one,
                backward_xk_low,
                backward_xv_low,
                backward_xr_low,
                backward_through,
                backward_numer_in,
                backward_denom_in,
                backward_transform_one,
                backward_tokens_one,
                backward_gate_one,
                backward_gated_low,
                backward_norm_two,
                backward_blend_two,
                backward_xk2_low,
                backward_xr2_low,
                backward_square_one,
                backward_squared_low,
                backward_branch_one,
            ) = records[level]
            d_recept, d_value_two = backward_branch_one(gradient)
            g_value_two = d_value_two.astype(jnp.bfloat16)
            g_recept = d_recept.astype(jnp.bfloat16)
            (d_key_two,) = backward_square_one(product_back(g_value_two, backward_w_fval))
            g_key_two = d_key_two.astype(jnp.bfloat16)
            d_hidden_two, d_edge_two, d_rates_two = backward_blend_two(
                (product_back(g_key_two, backward_w_fkey), product_back(g_recept, backward_w_frec))
            )
            d_hidden_two = d_hidden_two.at[:, -1, :].add(edge_back(d_edge_two))
            d_middle_norm, d_gain_two, d_bias_two = backward_norm_two(d_hidden_two)
            d_middle = gradient + d_middle_norm
            g_att = d_middle.astype(jnp.bfloat16)
            d_logit, d_mixed = backward_gate_one(product_back(g_att, backward_w_out))
            g_logit = d_logit.astype(jnp.bfloat16)
            (
                d_key_one,
                d_value_one,
                d_decay_one,
                d_first,
                backward_direct_numer,
                backward_direct_denom,
            ) = backward_tokens_one(d_mixed)
            chain_incoming = (empty, empty)
            chain_sent_numer = backward_direct_numer
            chain_sent_denom = backward_direct_denom
            for chain_relay_turn in range(lax.axis_size("seq") - 1):
                chain_incoming = from_behind((chain_sent_numer, chain_sent_denom), "seq", -1)
                chain_sent_numer = backward_through * chain_incoming[0] + backward_direct_numer
                chain_sent_denom = backward_through * chain_incoming[1] + backward_direct_denom
            g_numer_out, g_denom_out = chain_incoming
            d_key_two_part, d_value_two_part, d_decay_two = backward_transform_one(
                (
                    g_numer_out * backward_numer_in + g_denom_out * backward_denom_in,
                    g_numer_out,
                    g_denom_out,
                )
            )
            g_key = (d_key_one + d_key_two_part).astype(jnp.bfloat16)
            g_value = (d_value_one + d_value_two_part).astype(jnp.bfloat16)
            d_blends = (
                product_back(g_key, backward_w_kvr[:, :width]),
                product_back(g_value, backward_w_kvr[:, width : 2 * width]),
                product_back(g_logit, backward_w_kvr[:, 2 * width :]),
            )
            d_hidden, d_edge, d_rates = backward_blend_one(d_blends)
            d_hidden = d_hidden.at[:, -1, :].add(edge_back(d_edge))
            d_stream_norm, d_gain_one, d_bias_one = backward_norm_one(d_hidden)
            pairs = (
                (backward_xk2_low, g_key_two),
                (backward_xr2_low, g_recept),
                (backward_squared_low, g_value_two),
                (backward_xk_low, g_key),
                (backward_xv_low, g_value),
                (backward_xr_low, g_logit),
                (backward_gated_low, g_att),
            )
            columns = (
                [d_decay_one + d_decay_two, d_first]
                + [d_rates[j] for j in range(3)]
                + [d_rates_two[j] for j in range(2)]
                + [d_gain_one, d_gain_two, d_bias_one, d_bias_two]
            )
            backward_vectors = jnp.stack(columns, axis=1)
            gradient, pairs, vectors = (d_middle + d_stream_norm, pairs, backward_vectors)
            pair_lists[level].append(pairs)
            vector_sums[level] = (
                vectors if vector_sums[level] is None else vector_sums[level] + vectors
            )
        grad_parts.append(gradient.astype(jnp.bfloat16))
    results = [None] * layer_total
    for level in reversed(range(layer_total)):
        pair_list = pair_lists[level]

        def summed(index):
            inputs = jnp.concatenate([p[index][0] for p in pair_list], axis=0)
            grads = jnp.concatenate([p[index][1] for p in pair_list], axis=0)
            return outer_sum(inputs, grads)

        ffn_part = (summed(0), summed(1), summed(2))
        finish_grad_kvr = jnp.concatenate([summed(3), summed(4), summed(5)], axis=1)
        totals = (
            lax.psum(
                lax.psum_scatter(ffn_part[0], "dp", scatter_dimension=0, tiled=True).astype(
                    jnp.bfloat16
                ),
                "seq",
            ).astype(jnp.float32),
            lax.psum(
                lax.psum_scatter(ffn_part[1], "dp", scatter_dimension=0, tiled=True).astype(
                    jnp.bfloat16
                ),
                "seq",
            ).astype(jnp.float32),
            lax.psum(
                lax.psum_scatter(ffn_part[2], "dp", scatter_dimension=0, tiled=True).astype(
                    jnp.bfloat16
                ),
                "seq",
            ).astype(jnp.float32),
            lax.psum(
                lax.psum_scatter(finish_grad_kvr, "dp", scatter_dimension=0, tiled=True).astype(
                    jnp.bfloat16
                ),
                "seq",
            ).astype(jnp.float32),
            lax.psum(
                lax.psum_scatter(summed(6), "dp", scatter_dimension=0, tiled=True).astype(
                    jnp.bfloat16
                ),
                "seq",
            ).astype(jnp.float32),
            lax.psum(
                lax.psum_scatter(vector_sums[level], "dp", scatter_dimension=0, tiled=True).astype(
                    jnp.bfloat16
                ),
                "seq",
            ).astype(jnp.float32),
        )
        ffn_part = (totals[0], totals[1], totals[2])
        att_part = (totals[3], totals[4], totals[5])
        results[level] = (ffn_part, att_part)
    output = jnp.concatenate(outputs, axis=0)
    grad_tokens = jnp.concatenate(grad_parts, axis=0)
    grad_ffn_key = jnp.stack([r[0][0] for r in results])
    grad_ffn_recept = jnp.stack([r[0][1] for r in results])
    grad_ffn_value = jnp.stack([r[0][2] for r in results])
    grad_kvr = jnp.stack([r[1][0] for r in results])
    grad_att_out = jnp.stack([r[1][1] for r in results])
    vector_rows = jnp.stack([r[1][2] for r in results])
    grad_decay = vector_rows[:, :, 0]
    grad_first = vector_rows[:, :, 1]
    grad_mix = jnp.swapaxes(vector_rows[:, :, 2:7], 1, 2)
    grad_gain = jnp.swapaxes(vector_rows[:, :, 7:9], 1, 2)
    grad_bias = jnp.swapaxes(vector_rows[:, :, 9:11], 1, 2)
    return (
        output,
        grad_tokens,
        grad_decay,
        grad_first,
        grad_mix,
        grad_gain,
        grad_bias,
        grad_kvr,
        grad_att_out,
        grad_ffn_key,
        grad_ffn_recept,
        grad_ffn_value,
    )


def solution(mesh):
    in_specs = (
        P("dp", "seq", None),
        P("dp", None),
        P(),
        P(),
        P(),
        P(),
        P(),
        P(None, "dp", None),
        P(None, "dp", None),
        P(None, "dp", None),
        P(None, "dp", None),
        P(None, "dp", None),
        P("dp", "seq", None),
    )
    out_specs = (
        P("dp", "seq", None),
        P("dp", "seq", None),
        P(None, "dp"),
        P(None, "dp"),
        P(None, None, "dp"),
        P(None, None, "dp"),
        P(None, None, "dp"),
        P(None, "dp", None),
        P(None, "dp", None),
        P(None, "dp", None),
        P(None, "dp", None),
        P(None, "dp", None),
    )
    return jax.shard_map(body, mesh=mesh, in_specs=in_specs, out_specs=out_specs, check_vma=False)
```

profile of v0, /device:TPU:0, one launch (start us, length us, event | category | flops | bytes accessed | tf_op | source)
XLA Modules:
  0.0 1591.7 jit_solution(2875462977294792807)
XLA Ops:
  32.3 21.6 %all-gather.21.cloned.1.call-done = bf16[1,768,2304]{2,1,0:T(8,128)(2,1)} async-done(((bf16[1,96,2304]{2,1,0:T(8,128)(2,1)}), bf16[1,768,2304]{2,1,0:T(8,128)(2,1)}) %all-gather.21.cloned.1.call-update) | async-done | bytes 3538960 | tf_op jit(solution)/shard_map/all_gather | solution.py:224
  108.9 22.0 %all-gather.27.cloned.1.call-done = bf16[1,768,3072]{2,1,0:T(8,128)(2,1)} async-done(((bf16[1,96,3072]{2,1,0:T(8,128)(2,1)}), bf16[1,768,3072]{2,1,0:T(8,128)(2,1)}) %all-gather.27.cloned.1.call-update) | async-done | bytes 4718608 | tf_op jit(solution)/shard_map/all_gather | solution.py:226
  135.1 48.3 %all-gather.29.cloned.1.call-done = bf16[1,3072,768]{2,1,0:T(8,128)(2,1)} async-done(((bf16[1,384,768]{2,1,0:T(8,128)(2,1)}), bf16[1,3072,768]{2,1,0:T(8,128)(2,1)}) %all-gather.29.cloned.1.call-update) | async-done | bytes 4718608 | tf_op jit(solution)/shard_map/all_gather | solution.py:228
  187.1 19.4 %all-gather.25.cloned.1.call-done = bf16[1,768,768]{2,1,0:T(8,128)(2,1)} async-done(((bf16[1,96,768]{2,1,0:T(8,128)(2,1)}), bf16[1,768,768]{2,1,0:T(8,128)(2,1)}) %all-gather.25.cloned.1.call-update) | async-done | bytes 1179664 | tf_op jit(solution)/shard_map/all_gather | solution.py:227
  215.4 34.4 %all-gather.31.cloned.1.call-done = bf16[1,768,2304]{2,1,0:T(8,128)(2,1)} async-done(((bf16[1,96,2304]{2,1,0:T(8,128)(2,1)}), bf16[1,768,2304]{2,1,0:T(8,128)(2,1)}) %all-gather.31.cloned.1.call-update) | async-done | bytes 3538960 | tf_op jit(solution)/shard_map/all_gather | solution.py:224
  289.7 9.6 while.367
  311.1 15.7 all-gather.37.cloned.1.call-done
  331.1 48.5 %all-gather.39.cloned.1.call-done = bf16[1,3072,768]{2,1,0:T(8,128)(2,1)} async-done(((bf16[1,384,768]{2,1,0:T(8,128)(2,1)}), bf16[1,3072,768]{2,1,0:T(8,128)(2,1)}) %all-gather.39.cloned.1.call-update) | async-done | bytes 4718608 | tf_op jit(solution)/shard_map/all_gather | solution.py:228
  384.0 18.6 %all-gather.35.cloned.1.call-done = bf16[1,768,768]{2,1,0:T(8,128)(2,1)} async-done(((bf16[1,96,768]{2,1,0:T(8,128)(2,1)}), bf16[1,768,768]{2,1,0:T(8,128)(2,1)}) %all-gather.35.cloned.1.call-update) | async-done | bytes 1179664 | tf_op jit(solution)/shard_map/all_gather | solution.py:227
  424.8 17.3 %while.370 = (s32[]{:T(128)}, f32[64,768]{1,0:T(8,128)S(1)}, f32[64,768]{1,0:T(8,128)S(1)}, f32[64,768]{1,0:T(8,128)}, f32[768]{0:T(1024)S(1)}, /*index=5*/f32[7...) while((s32[]{:T(128)}, f32[64,768]{1,0:T(8,128)S(1)}, ...), condition=%wide.region_65.66_spmd.clone.clone.clone, body=%wide.region_61.65_spmd.clone.clone.clone.sunk | while | flops 77912064 | bytes 10435256 | solution.py:86
  505.9 14.7 while.371
  583.2 8.3 while.364
  655.7 11.0 while.365
  710.1 18.9 %while.368 = (s32[]{:T(128)}, f32[64,768]{1,0:T(8,128)S(1)}, f32[64,768]{1,0:T(8,128)}, f32[64,768]{1,0:T(8,128)}, f32[768]{0:T(1024)S(1)}, /*index=5*/f32[768]{...) while((s32[]{:T(128)}, f32[64,768]{1,0:T(8,128)S(1)}, ...), condition=%wide.region_47.48_spmd.clone.clone.clone, body=%wide.region_43.47_spmd.clone.clone.clone.sunk | while | flops 77912064 | bytes 12008176 | solution.py:86
  811.6 14.3 while.369
  930.2 72.4 %reduce-scatter.41.cloned.1.call-done = f32[96,2304]{1,0:T(8,128)} async-done(((f32[768,2304]{1,0:T(8,128)}), f32[96,2304]{1,0:T(8,128)}) %reduce-scatter.41.cloned.1.call-update) | async-done | bytes 884752
  1004.8 97.8 %reduce-scatter.35.cloned.1.call-done = f32[384,768]{1,0:T(8,128)} async-done(((f32[3072,768]{1,0:T(8,128)}), f32[384,768]{1,0:T(8,128)}) %reduce-scatter.35.cloned.1.call-update) | async-done | bytes 1179664 | tf_op jit(solution)/shard_map/reduce_scatter | solution.py:364
  1104.8 97.9 %reduce-scatter.27.cloned.1.call-done = f32[96,3072]{1,0:T(8,128)} async-done(((f32[768,3072]{1,0:T(8,128)}), f32[96,3072]{1,0:T(8,128)}) %reduce-scatter.27.cloned.1.call-update) | async-done | bytes 1179664 | tf_op jit(solution)/shard_map/reduce_scatter | solution.py:352
  1204.9 98.0 %reduce-scatter.25.cloned.1.call-done = f32[96,3072]{1,0:T(8,128)} async-done(((f32[768,3072]{1,0:T(8,128)}), f32[96,3072]{1,0:T(8,128)}) %reduce-scatter.25.cloned.1.call-update) | async-done | bytes 1179664 | tf_op jit(solution)/shard_map/reduce_scatter | solution.py:352
  1305.1 97.9 %reduce-scatter.33.cloned.1.call-done = f32[384,768]{1,0:T(8,128)} async-done(((f32[3072,768]{1,0:T(8,128)}), f32[384,768]{1,0:T(8,128)}) %reduce-scatter.33.cloned.1.call-update) | async-done | bytes 1179664 | tf_op jit(solution)/shard_map/reduce_scatter | solution.py:364
  1408.1 26.1 %reduce-scatter.39.cloned.1.call-done = f32[96,11]{1,0:T(8,128)} async-done(((f32[768,11]{1,0:T(8,128)}), f32[96,11]{1,0:T(8,128)}) %reduce-scatter.39.cloned.1.call-update) | async-done | bytes 4240
  1435.1 30.3 %reduce-scatter.37.cloned.1.call-done = f32[96,11]{1,0:T(8,128)} async-done(((f32[768,11]{1,0:T(8,128)}), f32[96,11]{1,0:T(8,128)}) %reduce-scatter.37.cloned.1.call-update) | async-done | bytes 4240
  1466.3 10.1 all-reduce.68
  1478.2 98.3 %all-reduce.72.cloned.1.call-done = (bf16[1,96,2304]{1,2,0:T(8,128)(2,1)}, bf16[1,96,2304]{1,2,0:T(8,128)(2,1)}, bf16[1,96,768]{2,1,0:T(8,128)(2,1)}, bf16[1,96,...) async-done(((bf16[1,96,2304]{1,2,0:T(8,128)(2,1)}, ...) | async-done | bytes 3833872 | tf_op jit(solution)/shard_map/psum | solution.py:369
  (2132 shorter events, 716.2 us)
Async XLA Ops:
  7.2 46.8 %all-gather.21.cloned.1.call-start = ((), (), s32[]{:S(2)}) async-start(), calls=%async_computation.20 | async-start | bytes 3981312 | tf_op jit(solution)/shard_map/all_gather | solution.py:224
  9.5 90.9 %all-gather.23.cloned.1.call-start = ((), (), s32[]{:S(2)}) async-start(), calls=%async_computation.21 | async-start | bytes 1327104 | tf_op jit(solution)/shard_map/all_gather | solution.py:225
  10.3 120.5 %all-gather.27.cloned.1.call-start = ((), (), s32[]{:S(2)}) async-start(), calls=%async_computation.23 | async-start | bytes 5308416 | tf_op jit(solution)/shard_map/all_gather | solution.py:226
  11.5 172.0 %all-gather.29.cloned.1.call-start = ((), (), s32[]{:S(2)}) async-start(), calls=%async_computation.24 | async-start | bytes 5308416 | tf_op jit(solution)/shard_map/all_gather | solution.py:228
  13.1 193.3 %all-gather.25.cloned.1.call-start = ((), (), s32[]{:S(2)}) async-start(), calls=%async_computation.22 | async-start | bytes 1327104 | tf_op jit(solution)/shard_map/all_gather | solution.py:227
  13.9 235.9 %all-gather.31.cloned.1.call-start = ((), (), s32[]{:S(2)}) async-start(), calls=%async_computation.25 | async-start | bytes 3981312 | tf_op jit(solution)/shard_map/all_gather | solution.py:224
  14.5 287.5 %all-gather.33.cloned.1.call-start = ((), (), s32[]{:S(2)}) async-start(), calls=%async_computation.26 | async-start | bytes 1327104 | tf_op jit(solution)/shard_map/all_gather | solution.py:225
  15.3 311.5 %all-gather.37.cloned.1.call-start = ((), (), s32[]{:S(2)}) async-start(), calls=%async_computation.28 | async-start | bytes 5308416 | tf_op jit(solution)/shard_map/all_gather | solution.py:226
  16.0 363.6 %all-gather.39.cloned.1.call-start = ((), (), s32[]{:S(2)}) async-start(), calls=%async_computation.29 | async-start | bytes 5308416 | tf_op jit(solution)/shard_map/all_gather | solution.py:228
  22.9 379.7 %all-gather.35.cloned.1.call-start = ((), (), s32[]{:S(2)}) async-start(), calls=%async_computation.27 | async-start | bytes 1327104 | tf_op jit(solution)/shard_map/all_gather | solution.py:227
  278.1 643.3 %reduce-scatter.31.cloned.1.call-start = ((), (), s32[]{:S(2)}) async-start(), calls=%async_computation.17 | async-start | bytes 2654208 | tf_op jit(solution)/shard_map/reduce_scatter | solution.py:358
  687.0 236.0 %reduce-scatter.23.cloned.1.call-start = ((), (), s32[]{:S(2)}) async-start(), calls=%async_computation.13 | async-start | bytes 2654208 | tf_op jit(solution)/shard_map/reduce_scatter | solution.py:376
  705.7 219.0 %reduce-scatter.29.cloned.1.call-start = ((), (), s32[]{:S(2)}) async-start(), calls=%async_computation.16 | async-start | bytes 2654208 | tf_op jit(solution)/shard_map/reduce_scatter | solution.py:358
  771.2 155.1 %reduce-scatter.21.cloned.1.call-start = ((), (), s32[]{:S(2)}) async-start(), calls=%async_computation.12 | async-start | bytes 2654208 | tf_op jit(solution)/shard_map/reduce_scatter | solution.py:376
  791.3 136.6 %reduce-scatter.43.cloned.1.call-start = ((), (), s32[]{:S(2)}) async-start(), calls=%async_computation.33 | async-start | bytes 7962624
  806.9 195.7 %reduce-scatter.41.cloned.1.call-start = ((), (), s32[]{:S(2)}) async-start(), calls=%async_computation.32 | async-start | bytes 7962624
  867.0 235.7 %reduce-scatter.35.cloned.1.call-start = ((), (), s32[]{:S(2)}) async-start(), calls=%async_computation.19 | async-start | bytes 10616832 | tf_op jit(solution)/shard_map/reduce_scatter | solution.py:364
  876.0 326.7 %reduce-scatter.27.cloned.1.call-start = ((), (), s32[]{:S(2)}) async-start(), calls=%async_computation.15 | async-start | bytes 10616832 | tf_op jit(solution)/shard_map/reduce_scatter | solution.py:352
  882.5 420.4 %reduce-scatter.25.cloned.1.call-start = ((), (), s32[]{:S(2)}) async-start(), calls=%async_computation.14 | async-start | bytes 10616832 | tf_op jit(solution)/shard_map/reduce_scatter | solution.py:352
  889.0 514.0 %reduce-scatter.33.cloned.1.call-start = ((), (), s32[]{:S(2)}) async-start(), calls=%async_computation.18 | async-start | bytes 10616832 | tf_op jit(solution)/shard_map/reduce_scatter | solution.py:364
  898.0 536.3 %reduce-scatter.39.cloned.1.call-start = ((), (), s32[]{:S(2)}) async-start(), calls=%async_computation.31 | async-start | bytes 442368
  905.4 9.9 collective-permute-start.63
  915.0 550.4 %reduce-scatter.37.cloned.1.call-start = ((), (), s32[]{:S(2)}) async-start(), calls=%async_computation.30 | async-start | bytes 442368
  921.3 655.1 %all-reduce.72.cloned.1.call-start = ((), (), s32[]{:S(2)}) async-start(), calls=%async_computation.34 | async-start | bytes 8257536 | tf_op jit(solution)/shard_map/psum | solution.py:369
  (652 other events, 6530.3 us)
Sparse Core Ops, SparseCore 0:
  9.7 44.2 all-gather.20
  55.6 21.4 all-gather.22
  79.3 51.4 all-gather.26
  132.9 50.5 all-gather.28
  185.0 21.4 all-gather.24
  208.5 41.2 all-gather.30
  251.5 21.5 all-gather.32
  275.3 51.4 all-gather.36
  329.0 50.5 all-gather.38
  381.1 21.4 all-gather.34
  687.1 36.2 reduce-scatter.30
  726.2 35.7 reduce-scatter.22
  771.3 36.5 reduce-scatter.28
  810.6 35.4 reduce-scatter.20
  848.2 76.5 reduce-scatter.42
  927.0 75.6 reduce-scatter.40
  1004.8 97.8 reduce-scatter.34
  1104.8 97.8 reduce-scatter.26
  1205.0 97.8 reduce-scatter.24
  1305.1 97.8 reduce-scatter.32
  1405.2 28.9 reduce-scatter.38
  1436.6 28.7 reduce-scatter.36
  1471.9 104.4 all-reduce.71
where the time goes:
time: 1610 us; the launch traced here: 1590 us
  waiting for transfers between devices  952 us (59%)
  starting transfers between devices  166 us (10%)
  matrix products  166 us (10%)
  other arithmetic  147 us (9%)
  local copies, waits for them, and re-layouts  125 us (8%)
  between operations  23.8 us (1%)
    reduce_scatter x2, waiting for transfers between devices, body(): lax.psum_scatter(ffn_part[0], 'dp', scatter_dimension=0, tiled=True)  196 us
    reduce_scatter x2, waiting for transfers between devices, body(): lax.psum_scatter(ffn_part[2], 'dp', scatter_dimension=0, tiled=True)  196 us
    ppermute x64, starting transfers between devices, from_behind(): return lax.ppermute(block, axis, route)  164 us
    unnamed x27, waiting for transfers between devices  131 us
    ppermute x64, waiting for transfers between devices, from_behind(): return lax.ppermute(block, axis, route)  102 us
    psum x1, waiting for transfers between devices, body(): lax.psum(lax.psum_scatter(finish_grad_kvr, 'dp', scatter_dimension=0, til...  98.3 us
    all_gather x2, waiting for transfers between devices, body(): lax.all_gather(ffn_value[level], 'dp', axis=0, tiled=True)  96.9 us
    dot_general x28, matrix products, product(): jnp.einsum('rcd,de->rce', inputs, matrix, preferred_element_type=jnp.floa...  62.3 us
  transfers between devices with their start and end apart: 87, of which 61 were waited for; matrix products, arithmetic and copies ran while one was open for 16% of the time, Pallas kernels for 0%

commit v1 on v0

--- a/solution.py
+++ b/solution.py
@@ -1,11 +1,148 @@
+import functools
 import math
 
 import jax
 import jax.numpy as jnp
 from jax import lax
+from jax.experimental import pallas as pl
+from jax.experimental.pallas import tpu as pltpu
 from jax.sharding import PartitionSpec as P
 
 EPSILON = 1e-05
+MESH = pl.DeviceIdType.MESH
+
+class Place:
+    def __init__(self, lines):
+        self.lines = lines
+        s = lax.axis_index("seq"); d = lax.axis_index("dp")
+        self.s, self.d = s, d
+        self.c, self.z = lax.rem(d, 2), d // 2
+        x, y = lax.rem(s, 2), s // 2
+        c = self.c
+        self.f = x * (1 - c) + y * c
+        self.g = y * (1 - c) + x * c
+        flip_x, flip_y = s + 1 - 2 * x, s + 2 - 4 * y
+        self.first = (flip_x * (1 - c) + flip_y * c, d)
+        self.second = (flip_y * (1 - c) + flip_x * c, d)
+        self.partner = (s, d + 1 - 2 * c)
+    def line(self, k):
+        return lax.rem(self.z + k + self.lines, self.lines)
+    def along(self, k):
+        return (self.s, self.line(k) * 2 + self.c)
+
+def remote(src, dst, ssem, rsem, dev):
+    return pltpu.make_async_remote_copy(src_ref=src, dst_ref=dst, send_sem=ssem, recv_sem=rsem, device_id=dev, device_id_type=MESH)
+
+
+def gather_ops(pos, w, box, u, send, recv, lines):
+    r0, rows, c0, cols = box
+    gh = pl.ds(pl.multiple_of(r0 + pos.g * (rows // 2), 16), rows // 2)
+    fh = pl.ds(pl.multiple_of(c0 + pos.f * (cols // 2), 128), cols // 2)
+    ar, ac = pl.ds(r0, rows), pl.ds(c0, cols)
+    stages = [[], [], [], []]
+    for k in range(1, lines):
+        own, far = (pos.z, pos.c, gh, fh), pos.line(-k)
+        stages[0].append(remote(w.at[own], w.at[own], send.at[u, k - 1], recv.at[u, k - 1], pos.along(k)))
+        j = lines - 1 + k - 1
+        at = (far, pos.c, gh, fh)
+        stages[1].append(remote(w.at[at], w.at[at], send.at[u, j], recv.at[u, j], pos.second))
+        j = 2 * (lines - 1) + k - 1
+        at = (far, pos.c, ar, fh)
+        stages[2].append(remote(w.at[at], w.at[at], send.at[u, j], recv.at[u, j], pos.first))
+    j = 3 * (lines - 1)
+    half = w.at[:, pos.c, ar, ac]
+    stages[3].append(remote(half, half, send.at[u, j], recv.at[u, j], pos.partner))
+    return stages
+
+
+def boxes(shapes, pieces):
+    units = []
+    for i, (rows, cols) in enumerate(shapes):
+        if rows % (32 * pieces) == 0:
+            step = rows // pieces
+            units += [(i, (j, step, 0, cols)) for j in range(0, rows, step)]
+        elif cols % (256 * pieces) == 0:
+            step = cols // pieces
+            units += [(i, (0, rows, j, step)) for j in range(0, cols, step)]
+        else:
+            units.append((i, (0, rows, 0, cols)))
+    return units
+
+
+def gather_kernel(lines, ahead, units, n, *refs):
+    shards, wholes, slots = refs[:n], refs[n : 2 * n], refs[2 * n : 3 * n]
+    send, recv, local, out = refs[3 * n :]
+    pos = Place(lines)
+    barrier = pltpu.get_barrier_semaphore()
+    peers = [pos.along(k) for k in range(1, lines)] + [pos.first, pos.second, pos.partner]
+    for peer in peers:
+        pl.semaphore_signal(barrier, inc=1, device_id=peer, device_id_type=MESH)
+    locals_ = [
+        pltpu.make_async_copy(shards[i], slots[i].at[pos.z, pos.c], local.at[i]) for i in range(n)
+    ]
+    for copy in locals_:
+        copy.start()
+    pl.semaphore_wait(barrier, len(peers))
+    for copy in locals_:
+        copy.wait()
+    stages = [gather_ops(pos, slots[i], box, u, send, recv, lines) for u, (i, box) in enumerate(units)]
+    count = len(units)
+    for u in range(min(ahead, count)):
+        for copy in stages[u][0]:
+            copy.start()
+    for turn in range(count + 3):
+        if turn + ahead < count:
+            for copy in stages[turn + ahead][0]:
+                copy.start()
+        for stage in range(4):
+            u = turn - stage
+            if 0 <= u < count:
+                for i, copy in enumerate(stages[u][stage]):
+                    copy.wait_recv()
+                    if stage < 2:
+                        stages[u][stage + 1][i].start()
+                    if stage == 2 and i == lines - 2:
+                        stages[u][3][0].start()
+    for u in range(count):
+        for stage in range(4):
+            for copy in stages[u][stage]:
+                copy.wait_send()
+    outs = [pltpu.make_async_copy(slots[i], wholes[i], out.at[i]) for i in range(n)]
+    for copy in outs:
+        copy.start()
+    for copy in outs:
+        copy.wait()
+
+
+def gather_weights(shards, lines):
+    n = len(shards)
+    units = boxes([w.shape for w in shards], 3)
+    copies = 3 * (lines - 1) + 1
+    return pl.pallas_call(
+        functools.partial(gather_kernel, lines, 2, units, n),
+        out_shape=[jax.ShapeDtypeStruct((lines, 2) + w.shape, w.dtype) for w in shards],
+        in_specs=[pl.BlockSpec(memory_space=pl.ANY)] * n,
+        out_specs=[pl.BlockSpec(memory_space=pl.ANY)] * n,
+        scratch_shapes=[pltpu.VMEM((lines, 2) + w.shape, w.dtype) for w in shards]
+        + [
+            pltpu.SemaphoreType.DMA((len(units), copies)),
+            pltpu.SemaphoreType.DMA((len(units), copies)),
+            pltpu.SemaphoreType.DMA((n,)),
+            pltpu.SemaphoreType.DMA((n,)),
+        ],
+        compiler_params=pltpu.CompilerParams(
+            collective_id=0, has_side_effects=True, vmem_limit_bytes=60 * 2**20
+        ),
+    )(*shards)
+
+
+def kernel_fits(shards):
+    pairs = lax.axis_size("dp")
+    return (
+        lax.axis_size("seq") == 4
+        and pairs == 8
+        and all(w.shape[0] % 32 == 0 and w.shape[1] % 256 == 0 for w in shards)
+    )
 
 
 def from_behind(block, axis, distance):
@@ -119,7 +256,7 @@
 ):
     row_total, token_total, width = tokens.shape
     layer_total = decay.shape[0]
-    batches = 2
+    batches = 1
     per_batch = row_total // batches
     positions = lax.axis_index("seq") * token_total + jnp.arange(token_total, dtype=jnp.int32)
     starts_all = jnp.any(doc_starts[:, :, None] == positions[None, None, :], axis=1).astype(
@@ -217,17 +354,15 @@
         )
         return (middle + branch, record)
 
-    gathered = []
-    for level in range(layer_total):
-        gathered.append(
-            (
-                lax.all_gather(att_kvr[level], "dp", axis=0, tiled=True),
-                lax.all_gather(att_out[level], "dp", axis=0, tiled=True),
-                lax.all_gather(ffn_key[level], "dp", axis=0, tiled=True),
-                lax.all_gather(ffn_recept[level], "dp", axis=0, tiled=True),
-                lax.all_gather(ffn_value[level], "dp", axis=0, tiled=True),
-            )
-        )
+    names = (att_kvr, att_out, ffn_key, ffn_recept, ffn_value)
+    shards = [w[level] for level in range(layer_total) for w in names]
+    if kernel_fits(shards):
+        wholes = gather_weights(shards, lax.axis_size("dp") // 2)
+        wholes = [w.reshape(-1, w.shape[-1]) for w in wholes]
+    else:
+        wholes = [lax.all_gather(w, "dp", axis=0, tiled=True) for w in shards]
+    count = len(names)
+    gathered = [tuple(wholes[level * count : (level + 1) * count]) for level in range(layer_total)]
     pair_lists = [[] for level in range(layer_total)]
     vector_sums = [None] * layer_total
     outputs = []
@@ -349,39 +484,27 @@
         finish_grad_kvr = jnp.concatenate([summed(3), summed(4), summed(5)], axis=1)
         totals = (
             lax.psum(
-                lax.psum_scatter(ffn_part[0], "dp", scatter_dimension=0, tiled=True).astype(
-                    jnp.bfloat16
-                ),
+                lax.psum_scatter(ffn_part[0].astype(jnp.bfloat16), "dp", scatter_dimension=0, tiled=True),
                 "seq",
             ).astype(jnp.float32),
             lax.psum(
-                lax.psum_scatter(ffn_part[1], "dp", scatter_dimension=0, tiled=True).astype(
-                    jnp.bfloat16
-                ),
+                lax.psum_scatter(ffn_part[1].astype(jnp.bfloat16), "dp", scatter_dimension=0, tiled=True),
                 "seq",
             ).astype(jnp.float32),
             lax.psum(
-                lax.psum_scatter(ffn_part[2], "dp", scatter_dimension=0, tiled=True).astype(
-                    jnp.bfloat16
-                ),
+                lax.psum_scatter(ffn_part[2].astype(jnp.bfloat16), "dp", scatter_dimension=0, tiled=True),
                 "seq",
             ).astype(jnp.float32),
             lax.psum(
-                lax.psum_scatter(finish_grad_kvr, "dp", scatter_dimension=0, tiled=True).astype(
-                    jnp.bfloat16
-                ),
+                lax.psum_scatter(finish_grad_kvr.astype(jnp.bfloat16), "dp", scatter_dimension=0, tiled=True),
                 "seq",
             ).astype(jnp.float32),
             lax.psum(
-                lax.psum_scatter(summed(6), "dp", scatter_dimension=0, tiled=True).astype(
-                    jnp.bfloat16
-                ),
+                lax.psum_scatter(summed(6).astype(jnp.bfloat16), "dp", scatter_dimension=0, tiled=True),
                 "seq",
             ).astype(jnp.float32),
             lax.psum(
-                lax.psum_scatter(vector_sums[level], "dp", scatter_dimension=0, tiled=True).astype(
-                    jnp.bfloat16
-                ),
+                lax.psum_scatter(vector_sums[level], "dp", scatter_dimension=0, tiled=True),
                 "seq",
             ).astype(jnp.float32),
         )

time: 1610 us -> 1280 us (0.80)
  waiting for transfers between devices: 952 us -> 523 us
  Pallas kernels: 0 us -> 144 us
  starting transfers between devices: 166 us -> 79.6 us
  matrix products: 166 us -> 97.3 us
  other arithmetic: 147 us -> 204 us
  local copies, waits for them, and re-layouts: 125 us -> 182 us
    all_gather x10 -> x0, waiting for transfers between devices: 229 us -> none  [the longest x2 96.9 us: body(): lax.all_gather(ffn_value[level], 'dp', axis=0, tiled=True)]
    pallas_call x0 -> x1, Pallas kernels: none -> 144 us  [gather_weights(): pl.pallas_call(functools.partial(gather_kernel, lines, 2, units, n), out_...]
    ppermute x64 -> x32, starting transfers between devices: 164 us -> 78.2 us  [from_behind(): return lax.ppermute(block, axis, route)]
    unnamed x27 -> x17, waiting for transfers between devices: 131 us -> 59.8 us
    ppermute x64 -> x32, waiting for transfers between devices: 102 us -> 38.6 us  [from_behind(): return lax.ppermute(block, axis, route)]
    reduce_scatter x8, waiting for transfers between devices: 392 us -> 333 us  [the longest x2 111 us: body(): lax.psum_scatter(ffn_part[2].astype(jnp.bfloat16), 'dp', scatter_dimensio...]
    dot_general x28 -> x14, matrix products: 53.4 us -> 17.3 us  [product_back(): jnp.einsum('rce,de->rcd', grads, matrix, preferred_element_type=jnp.float32)]
    dot_general x28 -> x14, matrix products: 62.3 us -> 28.8 us  [product(): jnp.einsum('rcd,de->rce', inputs, matrix, preferred_element_type=jnp.floa...]
  transfers between devices with their start and end apart: 87 -> 45, of which waited for: 61 -> 31; matrix products, arithmetic and copies ran while one was open for 16% -> 15% of each run, Pallas kernels for 0% -> 11%
where the time goes in v1:
time: 1280 us; the launch traced here: 1270 us
  waiting for transfers between devices  523 us (41%)
  other arithmetic  204 us (16%)
  local copies, waits for them, and re-layouts  182 us (14%)
  Pallas kernels  144 us (11%)
  matrix products  97.3 us (8%)
  starting transfers between devices  79.6 us (6%)
  between operations  19.4 us (2%)
  blocking collectives  16.3 us (1%)
    pallas_call x1, Pallas kernels, gather_weights(): pl.pallas_call(functools.partial(gather_kernel, lines, 2, units, n), out_...  144 us
    reduce_scatter x2, waiting for transfers between devices, body(): lax.psum_scatter(ffn_part[2].astype(jnp.bfloat16), 'dp', scatter_dimensio...  111 us
    reduce_scatter x2, waiting for transfers between devices, body(): lax.psum_scatter(ffn_part[0].astype(jnp.bfloat16), 'dp', scatter_dimensio...  111 us
    psum x1, waiting for transfers between devices, body(): lax.psum(lax.psum_scatter(finish_grad_kvr.astype(jnp.bfloat16), 'dp', sca...  91.4 us
    ppermute x32, starting transfers between devices, from_behind(): return lax.ppermute(block, axis, route)  78.2 us
    reduce_scatter x2, waiting for transfers between devices, body(): lax.psum_scatter(summed(6).astype(jnp.bfloat16), 'dp', scatter_dimension=...  66.8 us
    unnamed x17, waiting for transfers between devices  59.8 us
    reduce_scatter x2, waiting for transfers between devices, body(): lax.psum_scatter(ffn_part[1].astype(jnp.bfloat16), 'dp', scatter_dimensio...  43.6 us
  transfers between devices with their start and end apart: 45, of which 31 were waited for; matrix products, arithmetic and copies ran while one was open for 15% of the time, Pallas kernels for 11%

profile of v1, /device:TPU:0, one launch (start us, length us, event | category | flops | bytes accessed | tf_op | source)
XLA Modules:
  0.0 1266.3 jit_solution(2965981949388864827)
XLA Ops:
  12.5 4.8 collective-permute-start
  27.4 144.1 %shard_map.220 = (bf16[4,2,96,2304]{3,2,1,0:T(8,128)(2,1)}, bf16[4,2,96,768]{3,2,1,0:T(8,128)(2,1)}, bf16[4,2,96,3072]{3,2,1,0:T(8,128)(2,1)}, bf16[4,2,96,768]{...) custom-call(bf16[96,2304]{1,0:T(8,128)(2,1)} %get-tuple-element.4538, ...), custom_call_target="tpu_custom_call" | custom-call | tf_op jit(solution)/shard_map/pallas_call | solution.py:121
  189.3 4.7 collective-permute-start.5
  224.2 42.3 %while.182 = (s32[]{:T(128)}, f32[2,768]{1,0:T(2,128)}, f32[2,768]{1,0:T(2,128)}, f32[2,2,64,768]{3,1,2,0:T(2,128)}, f32[2,2,64,768]{3,1,2,0:T(2,128)}, /*index=...) while((s32[]{:T(128)}, f32[2,768]{1,0:T(2,128)}, ...), condition=%wide.region_9.10_spmd.clone.clone.clone, body=%wide.region_7.9_spmd.clone.clone.clone.sunk | while | flops 153083776 | bytes 29250100 | solution.py:223
  282.1 5.6 fusion.158
  350.5 43.8 %while.183 = (s32[]{:T(128)}, f32[2,768]{1,0:T(2,128)}, f32[2,768]{1,0:T(2,128)}, f32[2,2,64,768]{3,1,2,0:T(2,128)}, f32[2,2,64,768]{3,1,2,0:T(2,128)}, /*index=...) while((s32[]{:T(128)}, f32[2,768]{1,0:T(2,128)}, ...), condition=%wide.region_18.19_spmd.clone.clone.clone, body=%wide.region_16.18_spmd.clone.clone.clone.sunk | while | flops 153083776 | bytes 32420432 | solution.py:223
  417.4 4.9 fusion.183
  452.6 50.9 %while.184 = (s32[]{:T(128)}, f32[64,768]{1,0:T(8,128)}, f32[64,768]{1,0:T(8,128)}, f32[64,768]{1,0:T(8,128)}, f32[768]{0:T(1024)}, /*index=5*/f32[768]{0:T(1024...) while((s32[]{:T(128)}, f32[64,768]{1,0:T(8,128)}, ...), condition=%wide.region_34.35_spmd.clone.clone.clone, body=%wide.region_23.0_spmd.clone.clone.clone.sunk | while | flops 155281920 | bytes 47015236 | solution.py:223
  531.6 5.2 multiply_reduce_fusion.17
  544.7 5.8 copy.1163
  590.7 49.5 %while.185 = (s32[]{:T(128)}, f32[64,768]{1,0:T(8,128)}, f32[64,768]{1,0:T(8,128)}, f32[64,768]{1,0:T(8,128)}, f32[768]{0:T(1024)}, /*index=5*/f32[768]{0:T(1024...) while((s32[]{:T(128)}, f32[64,768]{1,0:T(8,128)}, ...), condition=%wide.region_50.51_spmd.clone.clone.clone, body=%wide.region_39.0_spmd.clone.clone.clone.sunk | while | flops 155281920 | bytes 47015236 | solution.py:223
  715.6 8.9 multiply_reduce_fusion.11
  744.8 10.4 reduce-scatter.31.cloned.1.call-done
  755.2 33.7 %reduce-scatter.23.cloned.1.call-done = bf16[96,768]{1,0:T(8,128)(2,1)} async-done(((bf16[768,768]{1,0:T(8,128)(2,1)}), bf16[96,768]{1,0:T(8,128)(2,1)}) %reduce-scatter.23.cloned.1.call-update) | async-done | bytes 147472 | tf_op jit(solution)/shard_map/reduce_scatter | solution.py:503
  788.9 33.2 %reduce-scatter.29.cloned.1.call-done = bf16[96,768]{1,0:T(8,128)(2,1)} async-done(((bf16[768,768]{1,0:T(8,128)(2,1)}), bf16[96,768]{1,0:T(8,128)(2,1)}) %reduce-scatter.29.cloned.1.call-update) | async-done | bytes 147472 | tf_op jit(solution)/shard_map/reduce_scatter | solution.py:491
  822.1 33.1 %reduce-scatter.21.cloned.1.call-done = bf16[96,768]{1,0:T(8,128)(2,1)} async-done(((bf16[768,768]{1,0:T(8,128)(2,1)}), bf16[96,768]{1,0:T(8,128)(2,1)}) %reduce-scatter.21.cloned.1.call-update) | async-done | bytes 147472 | tf_op jit(solution)/shard_map/reduce_scatter | solution.py:503
  855.2 55.6 %reduce-scatter.35.cloned.1.call-done = bf16[384,768]{1,0:T(8,128)(2,1)} async-done(((bf16[3072,768]{1,0:T(8,128)(2,1)}), bf16[384,768]{1,0:T(8,128)(2,1)}) %reduce-scatter.35.cloned.1.call-update) | async-done | bytes 589840 | tf_op jit(solution)/shard_map/reduce_scatter | solution.py:495
  910.9 55.6 %reduce-scatter.27.cloned.1.call-done = bf16[96,3072]{1,0:T(8,128)(2,1)} async-done(((bf16[768,3072]{1,0:T(8,128)(2,1)}), bf16[96,3072]{1,0:T(8,128)(2,1)}) %reduce-scatter.27.cloned.1.call-update) | async-done | bytes 589840 | tf_op jit(solution)/shard_map/reduce_scatter | solution.py:487
  966.5 55.7 %reduce-scatter.33.cloned.1.call-done = bf16[384,768]{1,0:T(8,128)(2,1)} async-done(((bf16[3072,768]{1,0:T(8,128)(2,1)}), bf16[384,768]{1,0:T(8,128)(2,1)}) %reduce-scatter.33.cloned.1.call-update) | async-done | bytes 589840 | tf_op jit(solution)/shard_map/reduce_scatter | solution.py:495
  1022.2 55.5 %reduce-scatter.25.cloned.1.call-done = bf16[96,3072]{1,0:T(8,128)(2,1)} async-done(((bf16[768,3072]{1,0:T(8,128)(2,1)}), bf16[96,3072]{1,0:T(8,128)(2,1)}) %reduce-scatter.25.cloned.1.call-update) | async-done | bytes 589840 | tf_op jit(solution)/shard_map/reduce_scatter | solution.py:487
  1080.2 28.8 %reduce-scatter.39.cloned.1.call-done = f32[96,11]{1,0:T(8,128)} async-done(((f32[768,11]{1,0:T(8,128)}), f32[96,11]{1,0:T(8,128)}) %reduce-scatter.39.cloned.1.call-update) | async-done | bytes 4240
  1109.9 30.7 %reduce-scatter.37.cloned.1.call-done = f32[96,11]{1,0:T(8,128)} async-done(((f32[768,11]{1,0:T(8,128)}), f32[96,11]{1,0:T(8,128)}) %reduce-scatter.37.cloned.1.call-update) | async-done | bytes 4240
  1141.5 16.3 %all-reduce.34 = (f32[1,96,11]{1,2,0:T(8,128)S(1)}, f32[1,96,11]{1,2,0:T(8,128)S(1)}) all-reduce(f32[1,96,11]{1,2,0:T(8,128)S(1)} %bitcast.826, f32[1,96,11]{1,2,0:T(8,128)S(1)} %bitcast.825), channel_id=1, replica_groups=mesh['seq'=4,'dp'=8] {'seq'}, use_global_device_ids=true, to_apply=%region_74.75 | all-reduce | flops 2112 | bytes 16896 | tf_op jit(solution)/shard_map/psum | solution.py:506
  1159.6 91.4 %all-reduce.38.cloned.1.call-done = (bf16[1,96,2304]{1,2,0:T(8,128)(2,1)}, bf16[1,96,2304]{1,2,0:T(8,128)(2,1)}, bf16[1,96,768]{2,1,0:T(8,128)(2,1)}, bf16[1,96,...) async-done(((bf16[1,96,2304]{1,2,0:T(8,128)(2,1)}, ...) | async-done | bytes 3833872 | tf_op jit(solution)/shard_map/psum | solution.py:498
  (1388 shorter events, 561.6 us)
Async XLA Ops:
  7.2 733.4 %reduce-scatter.43.cloned.1.call-start = ((), (), s32[]{:S(2)}) async-start(), calls=%async_computation.23 | async-start | bytes 3981312
  12.5 159.0 %collective-permute-start = (f32[2,768]{1,0:T(2,128)S(1)}, f32[2,768]{1,0:T(2,128)S(1)}, u32[]{:S(2)}, u32[]{:S(2)}) collective-permute-start(f32[2,768]{1,0:T(2,128)S(1)} %slice_bitcast_fusion.34), channel_id=1, source_target_pairs={{0,8},{8,16},{16,24},{1,9},{9,17},{17,25},{2,10},{10,18},{18,26},{... | collective-permute-start | bytes 18440 | tf_op jit(solution)/shard_map/ppermute | solution.py:151
  185.1 10.1 collective-permute-start.2
  195.4 12.2 collective-permute-start.3
  199.6 8.7 collective-permute-start.6
  303.4 7.9 collective-permute-start.12
  321.2 12.7 %collective-permute-start.11 = (f32[2,768]{1,0:T(2,128)S(1)}, f32[2,768]{1,0:T(2,128)S(1)}, u32[]{:S(2)}, u32[]{:S(2)}) collective-permute-start(f32[2,768]{1,0:T(2,128)S(1)} %get-tuple-element.4578), channel_id=1, source_target_pairs={{0,8},{8,16},{16,24},{1,9},{9,17},{17,25},{2,10},{10,18},{18,26},{... | collective-permute-start | bytes 18440 | tf_op jit(solution)/shard_map/ppermute | solution.py:151
  325.4 9.1 collective-permute-start.14
  539.6 11.5 collective-permute-start.23
  550.6 192.1 %reduce-scatter.41.cloned.1.call-start = ((), (), s32[]{:S(2)}) async-start(), calls=%async_computation.22 | async-start | bytes 3981312
  572.9 7.1 collective-permute-start.24
  641.8 7.2 collective-permute-start.28
  660.2 7.1 collective-permute-start.30
  674.7 80.5 %reduce-scatter.31.cloned.1.call-start = ((), (), s32[]{:S(2)}) async-start(), calls=%async_computation.17 | async-start | bytes 1327104 | tf_op jit(solution)/shard_map/reduce_scatter | solution.py:491
  677.4 111.5 %reduce-scatter.23.cloned.1.call-start = ((), (), s32[]{:S(2)}) async-start(), calls=%async_computation.13 | async-start | bytes 1327104 | tf_op jit(solution)/shard_map/reduce_scatter | solution.py:503
  679.0 143.1 %reduce-scatter.29.cloned.1.call-start = ((), (), s32[]{:S(2)}) async-start(), calls=%async_computation.16 | async-start | bytes 1327104 | tf_op jit(solution)/shard_map/reduce_scatter | solution.py:491
  681.9 173.4 %reduce-scatter.21.cloned.1.call-start = ((), (), s32[]{:S(2)}) async-start(), calls=%async_computation.12 | async-start | bytes 1327104 | tf_op jit(solution)/shard_map/reduce_scatter | solution.py:503
  684.6 226.3 %reduce-scatter.35.cloned.1.call-start = ((), (), s32[]{:S(2)}) async-start(), calls=%async_computation.19 | async-start | bytes 5308416 | tf_op jit(solution)/shard_map/reduce_scatter | solution.py:495
  688.4 278.1 %reduce-scatter.27.cloned.1.call-start = ((), (), s32[]{:S(2)}) async-start(), calls=%async_computation.15 | async-start | bytes 5308416 | tf_op jit(solution)/shard_map/reduce_scatter | solution.py:487
  692.9 329.3 %reduce-scatter.33.cloned.1.call-start = ((), (), s32[]{:S(2)}) async-start(), calls=%async_computation.18 | async-start | bytes 5308416 | tf_op jit(solution)/shard_map/reduce_scatter | solution.py:495
  698.5 379.2 %reduce-scatter.25.cloned.1.call-start = ((), (), s32[]{:S(2)}) async-start(), calls=%async_computation.14 | async-start | bytes 5308416 | tf_op jit(solution)/shard_map/reduce_scatter | solution.py:487
  703.9 405.1 %reduce-scatter.39.cloned.1.call-start = ((), (), s32[]{:S(2)}) async-start(), calls=%async_computation.21 | async-start | bytes 442368
  733.6 407.0 %reduce-scatter.37.cloned.1.call-start = ((), (), s32[]{:S(2)}) async-start(), calls=%async_computation.20 | async-start | bytes 442368
  740.5 510.4 %all-reduce.38.cloned.1.call-start = ((), (), s32[]{:S(2)}) async-start(), calls=%async_computation.24 | async-start | bytes 8257536 | tf_op jit(solution)/shard_map/psum | solution.py:498
  (399 other events, 4963.6 us)
Sparse Core Ops, SparseCore 0:
  550.7 48.8 reduce-scatter.42
  674.9 46.8 reduce-scatter.40
  724.0 31.1 reduce-scatter.30
  757.9 30.9 reduce-scatter.22
  791.0 31.0 reduce-scatter.28
  824.3 30.9 reduce-scatter.20
  857.5 53.2 reduce-scatter.34
  913.2 53.2 reduce-scatter.26
  968.8 53.3 reduce-scatter.32
  1024.3 53.3 reduce-scatter.24
  1079.9 29.0 reduce-scatter.38
  1111.8 28.7 reduce-scatter.36
  1146.5 104.3 all-reduce.37

commit v2 on v0

--- a/solution.py
+++ b/solution.py
@@ -1,11 +1,1052 @@
+import functools
 import math
 
 import jax
 import jax.numpy as jnp
 from jax import lax
+from jax.experimental import pallas as pl
+from jax.experimental.pallas import tpu as pltpu
 from jax.sharding import PartitionSpec as P
 
 EPSILON = 1e-05
+MESH = pl.DeviceIdType.MESH
+F32, LOW = jnp.float32, jnp.bfloat16
+
+
+class Place:
+    def __init__(self, lines):
+        self.lines = lines
+        s, d = lax.axis_index("seq"), lax.axis_index("dp")
+        self.s, self.d = s, d
+        self.c, self.z = lax.rem(d, 2), d // 2
+        x, y, c = lax.rem(s, 2), s // 2, self.c
+        self.f = x * (1 - c) + y * c
+        self.g = y * (1 - c) + x * c
+        flip_x, flip_y = s + 1 - 2 * x, s + 2 - 4 * y
+        self.first = (flip_x * (1 - c) + flip_y * c, d)
+        self.second = (flip_y * (1 - c) + flip_x * c, d)
+        self.across = (3 - s, d)
+        self.partner = (s, d + 1 - 2 * c)
+
+    def line(self, k):
+        return lax.rem(self.z + k + self.lines, self.lines)
+
+    def along(self, k):
+        return (self.s, self.line(k) * 2 + self.c)
+
+    def later(self, k):
+        return (self.s + k, self.d)
+
+
+def remote(src, dst, send, recv, device):
+    return pltpu.make_async_remote_copy(
+        src_ref=src, dst_ref=dst, send_sem=send, recv_sem=recv, device_id=device, device_id_type=MESH
+    )
+
+
+def signal(semaphore, device):
+    pl.semaphore_signal(semaphore, inc=1, device_id=device, device_id_type=MESH)
+
+
+def half(start, size, which, align):
+    return pl.ds(pl.multiple_of(start + which * (size // 2), align), size // 2)
+
+
+class Gather:
+    def __init__(self, pos, units, send, recv, ahead):
+        self.pos, self.units, self.ahead = pos, units, ahead
+        self.turns = 0
+        lines = pos.lines
+        self.stages = []
+        for u, (w, (r0, rows, c0, cols)) in enumerate(units):
+            gh, fh = half(r0, rows, pos.g, 16), half(c0, cols, pos.f, 128)
+            ar, ac = pl.ds(r0, rows), pl.ds(c0, cols)
+            stages = [[], [], [], []]
+            for k in range(1, lines):
+                far = pos.line(-k)
+                own = w.at[pos.z, pos.c, gh, fh]
+                stages[0].append(remote(own, own, send.at[u, k - 1], recv.at[u, k - 1], pos.along(k)))
+                j = lines - 1 + k - 1
+                block = w.at[far, pos.c, gh, fh]
+                stages[1].append(remote(block, block, send.at[u, j], recv.at[u, j], pos.second))
+                j = 2 * (lines - 1) + k - 1
+                block = w.at[far, pos.c, ar, fh]
+                stages[2].append(remote(block, block, send.at[u, j], recv.at[u, j], pos.first))
+            j = 3 * (lines - 1)
+            block = w.at[:, pos.c, ar, ac]
+            stages[3].append(remote(block, block, send.at[u, j], recv.at[u, j], pos.partner))
+            self.stages.append(stages)
+
+    def begin(self, u):
+        if u < len(self.units):
+            for copy in self.stages[u][0]:
+                copy.start()
+
+    def turn(self):
+        turn, count = self.turns, len(self.units)
+        self.turns += 1
+        self.begin(turn + self.ahead)
+        for stage in range(4):
+            u = turn - stage
+            if 0 <= u < count:
+                for i, copy in enumerate(self.stages[u][stage]):
+                    copy.wait_recv()
+                    if stage < 2:
+                        self.stages[u][stage + 1][i].start()
+                if stage == 2:
+                    self.stages[u][3][0].start()
+
+    def need(self, u):
+        while self.turns < u + 4:
+            self.turn()
+
+    def finish(self):
+        for stages in self.stages:
+            for stage in stages:
+                for copy in stage:
+                    copy.wait_send()
+
+
+class Reduce:
+    def __init__(self, pos, units, shared, send, recv, free, credit, local):
+        self.pos, self.units, self.shared = pos, units, shared
+        self.send, self.recv, self.free, self.credit, self.local = send, recv, free, credit, local
+        self.turns = 0
+        self.copies = {}
+
+    def copy(self, u, j, src, dst, device):
+        made = remote(src, dst, self.send.at[u, j], self.recv.at[u, j], device)
+        self.copies[u, j] = made
+        made.start()
+
+    def views(self, u):
+        w, landing, out, (r0, rows, c0, cols) = self.units[u]
+        pos = self.pos
+        v = {
+            "ar": pl.ds(r0, rows),
+            "ac": pl.ds(c0, cols),
+            "gh": half(r0, rows, pos.g, 16),
+            "go": half(r0, rows, 1 - pos.g, 16),
+            "fh": half(c0, cols, pos.f, 128),
+            "fo": half(c0, cols, 1 - pos.f, 128),
+            "r0": pl.ds(r0, rows // 2),
+            "r1": pl.ds(r0 + rows // 2, rows // 2),
+            "c0": pl.ds(c0, cols // 2),
+            "c1": pl.ds(c0 + cols // 2, cols // 2),
+        }
+        return w, landing, out, v
+
+    def emit(self, u):
+        w, landing, _, v = self.views(u)
+        pos = self.pos
+        if u >= self.shared:
+            pl.semaphore_wait(self.credit.at[u - self.shared], 1)
+        self.copy(
+            u, 0, w.at[:, 1 - pos.c, v["ar"], v["ac"]], landing.at[:, v["ar"], v["ac"]], pos.partner
+        )
+
+    def pair(self, u):
+        w, landing, _, v = self.views(u)
+        pos, c = self.pos, self.pos.c
+        self.copies[u, 0].wait_recv()
+
+        @pl.loop(0, pos.lines)
+        def _(z):
+            w[z, c, v["ar"], v["ac"]] += landing[z, v["ar"], v["ac"]]
+
+        if u < self.shared:
+            signal(self.credit.at[u], pos.partner)
+        self.copies[u, 0].wait_send()
+        signal(self.free.at[u, 0], pos.first)
+        signal(self.free.at[u, 1], pos.second)
+        for k in range(1, pos.lines):
+            signal(self.free.at[u, 1 + k], pos.along(-k))
+        pl.semaphore_wait(self.free.at[u, 0], 1)
+        self.copy(u, 1, w.at[:, c, v["ar"], v["fo"]], w.at[:, 1 - c, v["ar"], v["c0"]], pos.first)
+
+    def one(self, u):
+        w, _, _, v = self.views(u)
+        pos, c = self.pos, self.pos.c
+        self.copies[u, 1].wait_recv()
+
+        @pl.loop(0, pos.lines)
+        def _(z):
+            w[z, c, v["ar"], v["fh"]] += w[z, 1 - c, v["ar"], v["c0"]]
+
+        pl.semaphore_wait(self.free.at[u, 1], 1)
+        self.copy(u, 2, w.at[:, c, v["go"], v["fh"]], w.at[:, 1 - c, v["r0"], v["c1"]], pos.second)
+
+    def two(self, u):
+        w, _, _, v = self.views(u)
+        pos, c = self.pos, self.pos.c
+        self.copies[u, 2].wait_recv()
+
+        @pl.loop(0, pos.lines)
+        def _(z):
+            w[z, c, v["gh"], v["fh"]] += w[z, 1 - c, v["r0"], v["c1"]]
+
+        for k in range(1, pos.lines):
+            pl.semaphore_wait(self.free.at[u, 1 + k], 1)
+            self.copy(
+                u,
+                2 + k,
+                w.at[pos.line(k), c, v["gh"], v["fh"]],
+                w.at[k - 1, 1 - c, v["r1"], v["c1"]],
+                pos.along(k),
+            )
+
+    def line(self, u):
+        w, _, out, v = self.views(u)
+        pos, c, lines = self.pos, self.pos.c, self.pos.lines
+        for k in range(1, lines):
+            self.copies[u, 2 + k].wait_recv()
+        total = w[pos.z, c, v["gh"], v["fh"]].astype(F32)
+        for k in range(1, lines):
+            total = total + w[k - 1, 1 - c, v["r1"], v["c1"]].astype(F32)
+        w[pos.z, c, v["gh"], v["fh"]] = total.astype(LOW)
+        mine, there = w.at[pos.z, c, v["gh"], v["fh"]], out.at[v["gh"], v["fh"]]
+        pltpu.make_async_copy(mine, there, self.local.at[u]).start()
+        for j, device in enumerate((pos.first, pos.second, pos.across)):
+            self.copy(u, 2 + lines + j, mine, there, device)
+
+    def turn(self):
+        turn = self.turns
+        self.turns += 1
+        for stage, step in enumerate((self.pair, self.one, self.two, self.line)):
+            if 0 <= turn - stage < len(self.units):
+                step(turn - stage)
+
+    def finish(self):
+        lines = self.pos.lines
+        for u in range(len(self.units)):
+            w, _, out, v = self.views(u)
+            for j in range(1, 5 + lines):
+                self.copies[u, j].wait_send()
+            for j in range(2 + lines, 5 + lines):
+                self.copies[u, j].wait_recv()
+            mine, there = w.at[self.pos.z, self.pos.c, v["gh"], v["fh"]], out.at[v["gh"], v["fh"]]
+            pltpu.make_async_copy(mine, there, self.local.at[u]).wait()
+
+
+def dot(a, b):
+    return jnp.dot(a, b, preferred_element_type=F32)
+
+
+def dot_across(a, b):
+    return lax.dot_general(a, b, (((1,), (1,)), ((), ())), preferred_element_type=F32)
+
+
+SAVED = ("x", "x1", "key", "value", "logit", "numer", "denom", "value2", "recept")
+SAVED_LOW = ("xk", "xv", "xr", "gated", "xk2", "xr2")
+WIDE = 256
+BLOCK = 32
+VMEM_BYTES = 63 * 2**20
+
+
+def train_kernel(dims, *refs):
+    layers, lines, rows, length, width, hidden = dims
+    refs = list(refs)
+
+    def take(count):
+        got = refs[:count]
+        del refs[:count]
+        return got
+
+    matrices = 5
+    tokens, doc_starts, decay, first, mix, ln_gain, ln_bias = take(7)
+    shards = take(matrices)
+    (cotangent,) = take(1)
+    output, grad_tokens, vector_out = take(3)
+    grad_out = take(matrices)
+    names = SAVED + SAVED_LOW + ("squared",)
+    store = dict(zip(names, take(len(names))))
+    weights = [take(matrices) for _ in range(layers)]
+    landing = take(matrices)
+    act = dict(zip(names, take(len(names))))
+    (live, padded, grad, main, d_one, d_two, d_three, g_low, g_low2, g_low3, g_key2, turned) = take(12)
+    vectors, small, vec, v_buf = take(4)
+    (g_send, g_recv, own_sem, r_send, r_recv, r_free, r_credit, r_local, save_sem, load_sem, s_send, s_recv, v_send, v_recv) = take(14)
+    tokens_total = rows * length
+    blocks = length // BLOCK
+    chunk = length // 8
+    pos = Place(lines)
+    s, last = pos.s, 3
+
+    small[...] = jnp.zeros_like(small)
+    vectors[...] = jnp.zeros_like(vectors)
+    own = []
+    for l in range(layers):
+        for m in range(matrices):
+            own.append(
+                pltpu.make_async_copy(
+                    shards[m].at[l], weights[l][m].at[pos.z, pos.c], own_sem.at[l, m]
+                )
+            )
+    for copy in own:
+        copy.start()
+    barrier = pltpu.get_barrier_semaphore()
+    peers = [pos.along(k) for k in range(1, lines)]
+    peers += [pos.first, pos.second, pos.across, pos.partner]
+    for peer in peers:
+        signal(barrier, peer)
+    pl.semaphore_wait(barrier, len(peers))
+    for copy in own:
+        copy.wait()
+
+    def pieces(m, count):
+        _, _, r, c = weights[0][m].shape
+        if m == 4:
+            return [(m, (j * (r // count), r // count, 0, c)) for j in range(count)]
+        return [(m, (0, r, j * (c // count), c // count)) for j in range(count)]
+
+    layout = pieces(0, 3) + pieces(1, 1) + pieces(2, 3) + pieces(3, 1) + pieces(4, 3)
+    per_layer = len(layout)
+    gather = Gather(
+        pos,
+        [(weights[l][m], box) for l in range(layers) for m, box in layout],
+        g_send,
+        g_recv,
+        2,
+    )
+    for u in range(gather.ahead):
+        gather.begin(u)
+
+    kvr = pieces(0, 3)
+    back = pieces(4, 3) + pieces(3, 1) + pieces(2, 3) + pieces(1, 1) + [kvr[2], kvr[0], kvr[1]]
+    reduce = Reduce(
+        pos,
+        [
+            (weights[l][m], landing[m], grad_out[m].at[l], box)
+            for l in reversed(range(layers))
+            for m, box in back
+        ],
+        len(back),
+        r_send,
+        r_recv,
+        r_free,
+        r_credit,
+        r_local,
+    )
+
+    sub = lax.broadcasted_iota(jnp.int32, (8, width), 0)
+    place = lax.broadcasted_iota(jnp.int32, (length, 128), 0)
+    at_token = (place % 8) * chunk + place // 8 + s * length
+    for r in range(rows):
+        start = jnp.zeros((length, 128), F32)
+        for j in range(doc_starts.shape[1]):
+            start = jnp.where(at_token == doc_starts[r, j], 1.0, start)
+        live[r] = 1.0 - start
+    p_row = lax.broadcasted_iota(jnp.int32, (length, length), 0)
+    p_col = lax.broadcasted_iota(jnp.int32, (length, length), 1)
+    order = jnp.where((p_row % 8) * chunk + p_row // 8 == p_col, 1.0, 0.0).astype(LOW)
+    order_back = jnp.where((p_col % 8) * chunk + p_col // 8 == p_row, 1.0, 0.0).astype(LOW)
+
+    def spread(tile):
+        return jnp.concatenate([tile] * (width // 128), axis=-1)
+
+    def span(i):
+        return pl.ds(pl.multiple_of(i * BLOCK, BLOCK), BLOCK)
+
+    def span_on(i):
+        return pl.ds(pl.multiple_of(i * BLOCK + 8, 8), BLOCK)
+
+    def tile(i):
+        return pl.ds(pl.multiple_of(i * 8, 8), 8)
+
+    def flat(ref):
+        return ref[...].reshape(tokens_total, ref.shape[-1])
+
+    def wide(j, base=0, size=WIDE):
+        return pl.ds(pl.multiple_of(base + j * size, 128), size)
+
+    def fold(block):
+        return jnp.sum(block.reshape(rows * BLOCK // 8, 8, width), axis=0)
+
+    def add_vector(level, row, block):
+        vectors[level, row] += fold(block)
+
+    def saving(name, level):
+        if level == 0:
+            pltpu.make_async_copy(act[name], store[name], save_sem.at[names.index(name)]).start()
+
+    def saved(name, level):
+        if level == 1:
+            pltpu.make_async_copy(act[name], store[name], save_sem.at[names.index(name)]).wait()
+
+    def loading(some):
+        for name in some:
+            pltpu.make_async_copy(store[name], act[name], load_sem.at[names.index(name)]).start()
+
+    def loaded(name, level):
+        if level == 0:
+            pltpu.make_async_copy(store[name], act[name], load_sem.at[names.index(name)]).wait()
+
+    def hop(index, device):
+        return remote(small.at[0, index], small.at[1, index], s_send.at[index], s_recv.at[index], device)
+
+    edge_count = 4 * layers
+
+    def edge_start(index, step, there):
+        @pl.when(there)
+        def _():
+            hop(index, pos.later(step)).start()
+
+    def edge_wait(index, step, there):
+        @pl.when(there)
+        def _():
+            hop(index, pos.later(step)).wait_recv()
+
+    def edge_sent(index, step, there):
+        @pl.when(there)
+        def _():
+            hop(index, pos.later(step)).wait_send()
+
+    def chain_hop(level, direction, k):
+        slot = edge_count + (level * 2 + direction) * 3
+        return remote(
+            small.at[0, slot],
+            small.at[1, slot + k - 1],
+            s_send.at[slot + k - 1],
+            s_recv.at[slot + k - 1],
+            pos.later(k if direction == 0 else -k),
+        )
+
+    def chain_do(level, direction, what):
+        for k in range(1, 4):
+            inside = s + k <= last if direction == 0 else s - k >= 0
+            from_inside = s - k >= 0 if direction == 0 else s + k <= last
+
+            @pl.when(from_inside if what == "wait_recv" else inside)
+            def _():
+                getattr(chain_hop(level, direction, k), what)()
+
+    def chain_total(level, direction, r):
+        slot = edge_count + (level * 2 + direction) * 3
+        numer = jnp.zeros((1, width), F32)
+        denom = jnp.zeros((1, width), F32)
+        for k in (3, 2, 1):
+            through = small[1, slot + k - 1, 3 * r : 3 * r + 1, :]
+            numer = through * numer + small[1, slot + k - 1, 3 * r + 1 : 3 * r + 2, :]
+            denom = through * denom + small[1, slot + k - 1, 3 * r + 2 : 3 * r + 3, :]
+        return numer, denom
+
+    def centred(x):
+        center = x - jnp.mean(x, -1, keepdims=True)
+        spread_ = jnp.mean(center * center, -1, keepdims=True)
+        scale = lax.rsqrt(spread_ + EPSILON)
+        return center * scale, scale
+
+    def normalize_into(x_ref, level, which):
+        gain, bias = ln_gain[level, which : which + 1, :], ln_bias[level, which : which + 1, :]
+
+        @pl.loop(0, blocks)
+        def _(i):
+            n, _ = centred(x_ref[:, span(i), :])
+            padded[:, span_on(i), :] = n * gain + bias
+
+    def wrap_in(index):
+        for r in range(rows):
+            moved = pltpu.roll(padded[r, length : length + 8, :], 1, 0)
+            padded[r, 0:8, :] = jnp.where(sub == 0, small[1, index, r : r + 1, :], moved)
+
+    def normalize_shift(x_ref, level, which, outs, rates):
+        index = level * 2 + which
+        normalize_into(x_ref, level, which)
+        for r in range(rows):
+            small[0, index, r : r + 1, :] = padded[r, length + 7 : length + 8, :]
+        edge_start(index, 1, s < last)
+        edge_wait(index, 1, s > 0)
+        wrap_in(index)
+
+        @pl.loop(0, blocks)
+        def _(i):
+            h = padded[:, span_on(i), :]
+            before = padded[:, span(i), :] * spread(live[:, span(i), :])
+            for out, j in zip(outs, rates):
+                rate = mix[level, j : j + 1, :]
+                out[:, span(i), :] = (h * rate + before * (1.0 - rate)).astype(LOW)
+
+    def project(x_ref, w, base, count, put):
+        @pl.loop(0, count // WIDE)
+        def _(j):
+            block = w[:, :, :, wide(j, base)].reshape(-1, WIDE)
+            put(j, dot(flat(x_ref), block).reshape(rows, length, WIDE))
+
+    def put_in(ref):
+        def put(j, block):
+            ref[:, :, wide(j)] = block
+
+        return put
+
+    def back_project(g_ref, w, base, count, out_ref):
+        size = min(width, count)
+        for j in range(count // size):
+            block = w[:, :, :, base + j * size : base + (j + 1) * size].reshape(-1, size)
+            got = dot_across(g_ref[:, :, j * size : (j + 1) * size].reshape(tokens_total, size), block)
+            got = got.reshape(rows, length, width)
+            if j == 0:
+                out_ref[...] = got
+            else:
+                out_ref[...] += got
+
+    def outer(x_ref, g_ref, w, base, count, g_base=0):
+        turned[...] = flat(x_ref).T
+
+        @pl.loop(0, count // WIDE)
+        def _(j):
+            g = g_ref[:, :, wide(j, g_base)].reshape(tokens_total, WIDE)
+            got = dot(turned[...], g).astype(LOW)
+            w[:, :, :, wide(j, base)] = got.reshape(lines, 2, width // (2 * lines), WIDE)
+
+    def keep_rows(level):
+        rate = jnp.exp(decay[level : level + 1, :])
+        return jnp.broadcast_to(jnp.exp(-rate), (8, width)), rate
+
+    def scan_local(level):
+        keep, _ = keep_rows(level)
+
+        def step(i, carry):
+            out = []
+            for r in range(rows):
+                numer, denom, alive = carry[3 * r : 3 * r + 3]
+                l128 = live[r, tile(i), :]
+                l_now = spread(l128)
+                lifted = jnp.exp(act["key"][r, tile(i), :])
+                numer = keep * (numer * l_now) + lifted * act["value"][r, tile(i), :]
+                denom = keep * (denom * l_now) + lifted
+                out += [numer, denom, alive * l128]
+            return tuple(out)
+
+        zero = jnp.zeros((8, width), F32)
+        carry = lax.fori_loop(0, chunk, step, (zero, zero, jnp.ones((8, 128), F32)) * rows, unroll=2)
+        faded = keep
+        for _ in range(chunk.bit_length() - 1):
+            faded = faded * faded
+        slot = edge_count + (level * 2) * 3
+        before = []
+        for r in range(rows):
+            numer, denom, alive = carry[3 * r : 3 * r + 3]
+            through = spread(alive) * faded
+            vec[level, r] = through
+            for shift in (1, 2, 4):
+                inside = sub >= shift
+                n_b, d_b, t_b = (pltpu.roll(a, shift, 0) for a in (numer, denom, through))
+                numer = jnp.where(inside, through * n_b + numer, numer)
+                denom = jnp.where(inside, through * d_b + denom, denom)
+                through = jnp.where(inside, through * t_b, through)
+            for j, a in enumerate((through, numer, denom)):
+                small[0, slot, 3 * r + j : 3 * r + j + 1, :] = a[7:8, :]
+            at_start = sub == 0
+            n_b, d_b, t_b = (pltpu.roll(a, 1, 0) for a in (numer, denom, through))
+            before.append(
+                (jnp.where(at_start, 0.0, n_b), jnp.where(at_start, 0.0, d_b), jnp.where(at_start, 1.0, t_b))
+            )
+        chain_do(level, 0, "start")
+        return before
+
+    def scan_final(level, before):
+        chain_do(level, 0, "wait_recv")
+        keep, _ = keep_rows(level)
+        bonus = jnp.broadcast_to(jnp.exp(first[level : level + 1, :]), (8, width))
+        carry = []
+        for r in range(rows):
+            n_in, d_in = chain_total(level, 0, r)
+            n_b, d_b, t_b = before[r]
+            carry += [t_b * n_in + n_b, t_b * d_in + d_b]
+
+        def step(i, carry):
+            out = []
+            for r in range(rows):
+                numer, denom = carry[2 * r : 2 * r + 2]
+                l_now = spread(live[r, tile(i), :])
+                numer, denom = numer * l_now, denom * l_now
+                act["numer"][r, tile(i), :] = numer
+                act["denom"][r, tile(i), :] = denom
+                value = act["value"][r, tile(i), :]
+                lifted = jnp.exp(act["key"][r, tile(i), :])
+                now = bonus * lifted
+                main[r, tile(i), :] = (numer + now * value) / (denom + now)
+                out += [keep * numer + lifted * value, keep * denom + lifted]
+            return tuple(out)
+
+        lax.fori_loop(0, chunk, step, tuple(carry), unroll=2)
+
+    for r in range(rows):
+        act["x"][r] = dot(order, tokens[r])
+
+    def forward_layer(level):
+        w_kvr, w_out, w_fkey, w_frec, w_fval = weights[level]
+        base = level * per_layer
+        for name in ("xk", "xv", "xr"):
+            saved(name, level)
+        normalize_shift(act["x"], level, 0, [act["xk"], act["xv"], act["xr"]], (0, 1, 2))
+        saving("x", level)
+        for j, (low, name) in enumerate((("xk", "key"), ("xv", "value"), ("xr", "logit"))):
+            saving(low, level)
+            saved(name, level)
+            gather.need(base + j)
+            project(act[low], w_kvr, j * width, width, put_in(act[name]))
+            saving(name, level)
+            if j == 1:
+                before = scan_local(level)
+        saved("numer", level)
+        saved("denom", level)
+        scan_final(level, before)
+        saving("numer", level)
+        saving("denom", level)
+        saved("gated", level)
+
+        @pl.loop(0, blocks)
+        def _(i):
+            act["gated"][:, span(i), :] = (
+                jax.nn.sigmoid(act["logit"][:, span(i), :]) * main[:, span(i), :]
+            ).astype(LOW)
+
+        saving("gated", level)
+        gather.need(base + 3)
+        saved("x1", level)
+
+        def put_x1(j, block):
+            act["x1"][:, :, wide(j)] = act["x"][:, :, wide(j)] + block
+
+        project(act["gated"], w_out, 0, width, put_x1)
+        saving("x1", level)
+        saved("xk2", level)
+        saved("xr2", level)
+        normalize_shift(act["x1"], level, 1, [act["xk2"], act["xr2"]], (3, 4))
+        saving("xk2", level)
+        saving("xr2", level)
+        saved("squared", level)
+        third = hidden // 3
+        for j in range(3):
+            gather.need(base + 4 + j)
+
+            def put_squared(i, block, j=j):
+                up = jnp.maximum(block, 0.0)
+                act["squared"][:, :, wide(i, j * third)] = (up * up).astype(LOW)
+
+            project(act["xk2"], w_fkey, j * third, third, put_squared)
+        saving("squared", level)
+        gather.need(base + 7)
+        saved("recept", level)
+        project(act["xr2"], w_frec, 0, width, put_in(act["recept"]))
+        saving("recept", level)
+        gather.need(base + 10)
+        saved("value2", level)
+        share = hidden // lines
+        for j in range(width // WIDE):
+            total = None
+            for z in range(lines):
+                got = dot(
+                    act["squared"][:, :, z * share : (z + 1) * share].reshape(tokens_total, share),
+                    w_fval[z, :, :, j * WIDE : (j + 1) * WIDE].reshape(share, WIDE),
+                )
+                total = got if total is None else total + got
+            act["value2"][:, :, j * WIDE : (j + 1) * WIDE] = total.reshape(rows, length, WIDE)
+        saving("value2", level)
+        saved("x", level + 1)
+
+        @pl.loop(0, blocks)
+        def _(i):
+            up = jax.nn.sigmoid(act["recept"][:, span(i), :]) * act["value2"][:, span(i), :]
+            after = act["x1"][:, span(i), :] + up
+            if level + 1 < layers:
+                act["x"][:, span(i), :] = after
+            else:
+                g_low[:, span(i), :] = after.astype(LOW)
+
+    for level in range(layers):
+        forward_layer(level)
+    for r in range(rows):
+        output[r] = dot(order_back, g_low[r]).astype(LOW)
+        grad[r] = dot(order, cotangent[r])
+    gather.finish()
+
+    def blend_back(level, which, d_refs, rates):
+        index = level * 2 + which
+        wrap_in(index)
+
+        @pl.loop(0, blocks)
+        def _(i):
+            l_now = spread(live[:, span(i), :])
+            change = padded[:, span_on(i), :] - padded[:, span(i), :] * l_now
+            direct, shifted = None, None
+            for ref, j in zip(d_refs, rates):
+                d = ref[:, span(i), :]
+                rate = mix[level, j : j + 1, :]
+                add_vector(level, 2 + j, d * change)
+                direct = d * rate if direct is None else direct + d * rate
+                shifted = d * (1.0 - rate) if shifted is None else shifted + d * (1.0 - rate)
+            main[:, span(i), :] = direct
+            d_refs[0][:, span(i), :] = shifted * l_now
+
+        back_index = 2 * layers + index
+        for r in range(rows):
+            small[0, back_index, r : r + 1, :] = d_refs[0][r, 0:1, :]
+        edge_start(back_index, -1, s > 0)
+
+    def normalize_back(level, which, x_ref, q_ref, write):
+        index = level * 2 + which
+        back_index = 2 * layers + index
+        edge_wait(back_index, -1, s < last)
+        for r in range(rows):
+            moved = pltpu.roll(q_ref[r, 0:8, :], 7, 0)
+            padded[r, length : length + 8, :] = jnp.where(
+                sub == 7, small[1, back_index, r : r + 1, :], moved
+            )
+            padded[r, 8:length, :] = q_ref[r, 8:length, :]
+        gain = ln_gain[level, which : which + 1, :]
+
+        @pl.loop(0, blocks)
+        def _(i):
+            d_h = main[:, span(i), :] + padded[:, span_on(i), :]
+            n, scale = centred(x_ref[:, span(i), :])
+            add_vector(level, 7 + which, d_h * n)
+            add_vector(level, 9 + which, d_h)
+            e = d_h * gain
+            inner = e - jnp.mean(e, -1, keepdims=True) - n * jnp.mean(e * n, -1, keepdims=True)
+            after = grad[:, span(i), :] + scale * inner
+            grad[:, span(i), :] = after
+            write(i, after)
+
+    def wkv_terms(r, i, bonus):
+        value = act["value"][r, tile(i), :]
+        lifted = jnp.exp(act["key"][r, tile(i), :])
+        now = bonus * lifted
+        numer, denom = act["numer"][r, tile(i), :], act["denom"][r, tile(i), :]
+        part = 1.0 / (denom + now)
+        result = (numer + now * value) * part
+        return value, lifted, now, numer, denom, part, result
+
+    def scan_back_local(level):
+        keep, _ = keep_rows(level)
+        bonus = jnp.broadcast_to(jnp.exp(first[level : level + 1, :]), (8, width))
+
+        def step(j, carry):
+            i = chunk - 1 - j
+            out = []
+            for r in range(rows):
+                h_n, h_d = carry[2 * r : 2 * r + 2]
+                value, lifted, now, numer, denom, part, result = wkv_terms(r, i, bonus)
+                gate = jax.nn.sigmoid(act["logit"][r, tile(i), :])
+                d_gated = main[r, tile(i), :]
+                d_wkv = d_gated * gate
+                d_two[r, tile(i), :] = d_gated * result * gate * (1.0 - gate)
+                main[r, tile(i), :] = d_wkv
+                l_now = spread(live[r, tile(i), :])
+                a = d_wkv * part
+                out += [l_now * (a + keep * h_n), l_now * (keep * h_d - a * result)]
+            return tuple(out)
+
+        zero = jnp.zeros((8, width), F32)
+        carry = lax.fori_loop(0, chunk, step, (zero, zero) * rows)
+        slot = edge_count + (level * 2 + 1) * 3
+        after = []
+        for r in range(rows):
+            h_n, h_d = carry[2 * r : 2 * r + 2]
+            through = vec[level, r]
+            for shift in (1, 2, 4):
+                inside = sub < 8 - shift
+                n_a, d_a, t_a = (pltpu.roll(a, 8 - shift, 0) for a in (h_n, h_d, through))
+                h_n = jnp.where(inside, through * n_a + h_n, h_n)
+                h_d = jnp.where(inside, through * d_a + h_d, h_d)
+                through = jnp.where(inside, through * t_a, through)
+            for j, a in enumerate((through, h_n, h_d)):
+                small[0, slot, 3 * r + j : 3 * r + j + 1, :] = a[0:1, :]
+            at_end = sub == 7
+            n_a, d_a, t_a = (pltpu.roll(a, 7, 0) for a in (h_n, h_d, through))
+            after.append(
+                (jnp.where(at_end, 0.0, n_a), jnp.where(at_end, 0.0, d_a), jnp.where(at_end, 1.0, t_a))
+            )
+        chain_do(level, 1, "start")
+        return after
+
+    def scan_back_final(level, after):
+        chain_do(level, 1, "wait_recv")
+        keep, rate = keep_rows(level)
+        bonus = jnp.broadcast_to(jnp.exp(first[level : level + 1, :]), (8, width))
+        zero = jnp.zeros((8, width), F32)
+        carry = [zero, zero]
+        for r in range(rows):
+            n_in, d_in = chain_total(level, 1, r)
+            n_a, d_a, t_a = after[r]
+            carry += [t_a * n_in + n_a, t_a * d_in + d_a]
+
+        def step(j, carry):
+            i = chunk - 1 - j
+            d_keep, d_first = carry[:2]
+            out = []
+            for r in range(rows):
+                h_n, h_d = carry[2 + 2 * r : 4 + 2 * r]
+                value, lifted, now, numer, denom, part, result = wkv_terms(r, i, bonus)
+                a = main[r, tile(i), :] * part
+                d_now = a * (value - result) * now
+                d_keep = d_keep + numer * h_n + denom * h_d
+                d_first = d_first + d_now
+                d_one[r, tile(i), :] = d_now + lifted * (value * h_n + h_d)
+                d_two[r, tile(i), :] = a * now + lifted * h_n
+                l_now = spread(live[r, tile(i), :])
+                out += [l_now * (a + keep * h_n), l_now * (keep * h_d - a * result)]
+            return (d_keep, d_first, *out)
+
+        carry = lax.fori_loop(0, chunk, step, tuple(carry))
+        vectors[level, 0] += carry[0] * (-rate * keep)
+        vectors[level, 1] += carry[1]
+
+    def to_low(src, dst):
+        @pl.loop(0, blocks)
+        def _(i):
+            dst[:, span(i), :] = src[:, span(i), :].astype(LOW)
+
+    ffn_names = ("value2", "recept", "squared", "xk2", "xr2", "x1")
+    att_names = tuple(n for n in names if n not in ffn_names)
+
+    def backward_layer(level):
+        w_kvr, w_out, w_fkey, w_frec, w_fval = weights[level]
+        base = (layers - 1 - level) * per_layer
+        third = hidden // 3
+        share = hidden // lines
+        loaded("value2", level)
+        loaded("recept", level)
+
+        @pl.loop(0, blocks)
+        def _(i):
+            gate = jax.nn.sigmoid(act["recept"][:, span(i), :])
+            g = grad[:, span(i), :]
+            g_low[:, span(i), :] = (g * gate).astype(LOW)
+            g_low2[:, span(i), :] = (g * act["value2"][:, span(i), :] * gate * (1.0 - gate)).astype(LOW)
+
+        loaded("squared", level)
+
+        @pl.loop(0, lines)
+        def _(z):
+            got = dot_across(flat(g_low), w_fval[z].reshape(share, width)).reshape(rows, length, share)
+            root = jnp.sqrt(act["squared"][:, :, wide(z, 0, share)].astype(F32))
+            g_key2[:, :, wide(z, 0, share)] = (got * (2.0 * root)).astype(LOW)
+
+        @pl.loop(0, lines)
+        def _(z):
+            turned[...] = act["squared"][:, :, wide(z, 0, share)].reshape(tokens_total, share).T
+            for j in range(width // WIDE):
+                g = g_low[:, :, j * WIDE : (j + 1) * WIDE].reshape(tokens_total, WIDE)
+                got = dot(turned[...], g).astype(LOW)
+                w_fval[z, :, :, j * WIDE : (j + 1) * WIDE] = got.reshape(2, share // 2, WIDE)
+
+        for j in range(3):
+            reduce.emit(base + j)
+        loaded("xr2", level)
+        back_project(g_low2, w_frec, 0, width, d_two)
+        outer(act["xr2"], g_low2, w_frec, 0, width)
+        reduce.emit(base + 3)
+        reduce.turn()
+        back_project(g_key2, w_fkey, 0, hidden, d_one)
+        reduce.turn()
+        loaded("xk2", level)
+        for j in range(3):
+            outer(act["xk2"], g_key2, w_fkey, j * third, third, j * third)
+            reduce.emit(base + 4 + j)
+        loaded("x1", level)
+        normalize_into(act["x1"], level, 1)
+        blend_back(level, 1, [d_one, d_two], (3, 4))
+        reduce.turn()
+
+        def write_att(i, after):
+            g_low3[:, span(i), :] = after.astype(LOW)
+
+        normalize_back(level, 1, act["x1"], d_one, write_att)
+        if level == 1:
+            loading(ffn_names)
+        back_project(g_low3, w_out, 0, width, main)
+        loaded("gated", level)
+        outer(act["gated"], g_low3, w_out, 0, width)
+        reduce.emit(base + 7)
+        reduce.turn()
+        for name in ("logit", "key", "value", "numer", "denom"):
+            loaded(name, level)
+        after = scan_back_local(level)
+        to_low(d_two, g_low)
+        reduce.turn()
+        loaded("xr", level)
+        back_project(g_low, w_kvr, 2 * width, width, d_three)
+        outer(act["xr"], g_low, w_kvr, 2 * width, width)
+        reduce.emit(base + 8)
+        scan_back_final(level, after)
+        to_low(d_one, g_low2)
+        to_low(d_two, g_low3)
+        reduce.turn()
+        loaded("xk", level)
+        loaded("xv", level)
+        back_project(g_low2, w_kvr, 0, width, d_one)
+        outer(act["xk"], g_low2, w_kvr, 0, width)
+        reduce.emit(base + 9)
+        back_project(g_low3, w_kvr, width, width, d_two)
+        outer(act["xv"], g_low3, w_kvr, width, width)
+        reduce.emit(base + 10)
+        reduce.turn()
+        loaded("x", level)
+        normalize_into(act["x"], level, 0)
+        blend_back(level, 0, [d_one, d_two, d_three], (0, 1, 2))
+
+        def write_none(i, after):
+            g_low[:, span(i), :] = after.astype(LOW)
+
+        normalize_back(level, 0, act["x"], d_one, write_none)
+        if level == 1:
+            loading(att_names)
+
+    for level in reversed(range(layers)):
+        backward_layer(level)
+    for r in range(rows):
+        grad_tokens[r] = dot(order_back, g_low[r]).astype(LOW)
+
+    count = vectors.shape[1]
+
+    def vector_hop(j, device):
+        source = min(j, 3)
+        return remote(v_buf.at[0, source], v_buf.at[1, j], v_send.at[j], v_recv.at[j], device)
+
+    def vector_stage(stage):
+        if stage == 0:
+            for level in range(layers):
+                for row in range(count):
+                    j = level * count + row
+                    v_buf[0, 0, j : j + 1, :] = jnp.sum(vectors[level, row], axis=0, keepdims=True)
+        elif stage < 4:
+            vector_hop(stage - 1, pos.partner).wait_recv()
+            v_buf[0, stage] = v_buf[0, stage - 1] + v_buf[1, stage - 1]
+        if stage < 3:
+            vector_hop(stage, (pos.partner, pos.first, pos.second)[stage]).start()
+        elif stage == 3:
+            for k in range(1, lines):
+                vector_hop(2 + k, pos.along(k)).start()
+        else:
+            total = v_buf[0, 3]
+            for k in range(1, lines):
+                vector_hop(2 + k, pos.along(k)).wait_recv()
+                total = total + v_buf[1, 2 + k]
+            vector_out[...] = total
+
+    for stage in range(5):
+        vector_stage(stage)
+        if reduce.turns < len(reduce.units) + 3:
+            reduce.turn()
+    while reduce.turns < len(reduce.units) + 3:
+        reduce.turn()
+    reduce.finish()
+    for j, device in enumerate((pos.partner, pos.first, pos.second)):
+        vector_hop(j, device).wait_send()
+    for k in range(1, lines):
+        vector_hop(2 + k, pos.along(k)).wait_send()
+    for level in range(layers):
+        for which in range(2):
+            index = level * 2 + which
+            edge_sent(index, 1, s < last)
+            edge_sent(2 * layers + index, -1, s > 0)
+        for direction in range(2):
+            chain_do(level, direction, "wait_send")
+
+
+def fast_body(
+    tokens, doc_starts, decay, first, mix, ln_gain, ln_bias,
+    att_kvr, att_out, ffn_key, ffn_recept, ffn_value, cotangent,
+):
+    rows, length, width = tokens.shape
+    layers, hidden = decay.shape[0], ffn_key.shape[2]
+    lines = lax.axis_size("dp") // 2
+    shards = (att_kvr, att_out, ffn_key, ffn_recept, ffn_value)
+    plain, low = (rows, length, width), LOW
+    saved = [jax.ShapeDtypeStruct(plain, F32)] * len(SAVED)
+    saved += [jax.ShapeDtypeStruct(plain, low)] * len(SAVED_LOW)
+    saved += [jax.ShapeDtypeStruct((rows, length, hidden), low)]
+    vector_rows = -(-layers * 11 // 8) * 8
+    outs = [
+        jax.ShapeDtypeStruct(plain, low),
+        jax.ShapeDtypeStruct(plain, low),
+        jax.ShapeDtypeStruct((vector_rows, width), F32),
+    ]
+    outs += [jax.ShapeDtypeStruct(w.shape, low) for w in shards]
+    outs += saved
+    vmem, anywhere = pl.BlockSpec(memory_space=pltpu.VMEM), pl.BlockSpec(memory_space=pl.ANY)
+    units = 11 * layers
+    hops = 4 * layers + 6 * layers
+    dma, plain_f32, plain_low = pltpu.SemaphoreType.DMA, pltpu.VMEM(plain, F32), pltpu.VMEM(plain, low)
+    scratch = [pltpu.VMEM((lines, 2) + w.shape[1:], low) for _ in range(layers) for w in shards]
+    scratch += [pltpu.VMEM((lines,) + w.shape[1:], low) for w in shards]
+    scratch += [pltpu.VMEM(a.shape, a.dtype) for a in saved]
+    scratch += [
+        pltpu.VMEM((rows, length, 128), F32),
+        pltpu.VMEM((rows, length + 8, width), F32),
+        plain_f32,
+        plain_f32,
+        plain_f32,
+        plain_f32,
+        plain_f32,
+        plain_low,
+        plain_low,
+        plain_low,
+        pltpu.VMEM((rows, length, hidden), low),
+        pltpu.VMEM((width, rows * length), low),
+        pltpu.VMEM((layers, 11, 8, width), F32),
+        pltpu.VMEM((2, hops, 8, width), F32),
+        pltpu.VMEM((layers, rows, 8, width), F32),
+        pltpu.VMEM((2, 6, vector_rows, width), F32),
+        dma((units, 3 * lines - 2)),
+        dma((units, 3 * lines - 2)),
+        dma((layers, len(shards))),
+        dma((units, 5 + lines)),
+        dma((units, 5 + lines)),
+        pltpu.SemaphoreType.REGULAR((units, 1 + lines)),
+        pltpu.SemaphoreType.REGULAR((units // layers,)),
+        dma((units,)),
+        dma((len(saved),)),
+        dma((len(saved),)),
+        dma((hops,)),
+        dma((hops,)),
+        dma((6,)),
+        dma((6,)),
+    ]
+    smem = pl.BlockSpec(memory_space=pltpu.SMEM)
+    got = pl.pallas_call(
+        functools.partial(train_kernel, (layers, lines, rows, length, width, hidden)),
+        out_shape=outs,
+        in_specs=[vmem, smem] + [vmem] * 5 + [anywhere] * len(shards) + [vmem],
+        out_specs=[vmem] * 3 + [anywhere] * (len(outs) - 3),
+        scratch_shapes=scratch,
+        compiler_params=pltpu.CompilerParams(
+            collective_id=0, has_side_effects=True, vmem_limit_bytes=VMEM_BYTES
+        ),
+    )(tokens, doc_starts, decay, first, mix, ln_gain, ln_bias, *shards, cotangent)
+    output, grad_tokens, sums = got[:3]
+    share = width // lax.axis_size("dp")
+    sums = lax.dynamic_slice_in_dim(sums, lax.axis_index("dp") * share, share, axis=1)
+    sums = sums[: layers * 11].reshape(layers, 11, share)
+    return (
+        output,
+        grad_tokens,
+        sums[:, 0],
+        sums[:, 1],
+        sums[:, 2:7],
+        sums[:, 7:9],
+        sums[:, 9:11],
+        *[g.astype(F32) for g in got[3 : 3 + len(shards)]],
+    )
+
+
+def kernel_fits(tokens, decay, ffn_key, shards):
+    rows, length, width = tokens.shape
+    lines = lax.axis_size("dp") // 2
+    return (
+        lax.axis_size("seq") == 4
+        and lax.axis_size("dp") == 2 * lines
+        and lines > 1
+        and decay.shape[0] == 2
+        and rows == 2
+        and length % BLOCK == 0
+        and length & (length - 1) == 0
+        and width % WIDE == 0
+        and ffn_key.shape[2] == width * lines
+        and all(w.shape[1] % 32 == 0 and w.shape[2] % WIDE == 0 for w in shards)
+    )
 
 
 def from_behind(block, axis, distance):
@@ -117,6 +1158,11 @@
     ffn_value,
     cotangent,
 ):
+    shards = (att_kvr, att_out, ffn_key, ffn_recept, ffn_value)
+    if kernel_fits(tokens, decay, ffn_key, shards):
+        return fast_body(
+            tokens, doc_starts, decay, first, mix, ln_gain, ln_bias, *shards, cotangent
+        )
     row_total, token_total, width = tokens.shape
     layer_total = decay.shape[0]
     batches = 2

time: 1610 us -> 349 us (0.22); the launches traced: 1590 us -> 349 us
  waiting for transfers between devices: 952 us -> 0 us
  Pallas kernels: 0 us -> 335 us
  matrix products: 166 us -> 0 us
  starting transfers between devices: 166 us -> 0 us
  other arithmetic: 147 us -> 7.64 us
  local copies, waits for them, and re-layouts: 125 us -> 5.48 us
  between operations: 23.8 us -> 0.67 us
    reduce_scatter x8 -> x0, waiting for transfers between devices: 392 us -> none  [the longest x2 196 us: body(): lax.psum_scatter(ffn_part[0], 'dp', scatter_dimension=0, tiled=True)]
    pallas_call x0 -> x1, Pallas kernels: none -> 335 us  [fast_body(): pl.pallas_call(functools.partial(train_kernel, (layers, lines, rows, leng...]
    all_gather x10 -> x0, waiting for transfers between devices: 229 us -> none  [the longest x2 96.9 us: body(): lax.all_gather(ffn_value[level], 'dp', axis=0, tiled=True)]
    dot_general x102 -> x0, matrix products: 166 us -> none  [the longest x28 62.3 us: product(): jnp.einsum('rcd,de->rce', inputs, matrix, preferred_element_type=jnp.floa...]
    ppermute x64 -> x0, starting transfers between devices: 164 us -> none  [from_behind(): return lax.ppermute(block, axis, route)]
    unnamed x27 -> x0, waiting for transfers between devices: 131 us -> none
    ppermute x64 -> x0, waiting for transfers between devices: 102 us -> none  [from_behind(): return lax.ppermute(block, axis, route)]
    psum x1 -> x0, waiting for transfers between devices: 98.3 us -> none  [body(): lax.psum(lax.psum_scatter(finish_grad_kvr, 'dp', scatter_dimension=0, til...]
  transfers between devices with their start and end apart: 87 -> 0, of which waited for: 61 -> 0; matrix products, arithmetic and copies ran while one was open for 16% -> 0% of each run, Pallas kernels for 0% -> 0%
where the time goes in v2:
time: 349 us
  Pallas kernels  335 us (96%)
  other arithmetic  7.64 us (2%)
  local copies, waits for them, and re-layouts  5.48 us (2%)
    pallas_call x1, Pallas kernels, fast_body(): pl.pallas_call(functools.partial(train_kernel, (layers, lines, rows, leng...  335 us
    convert_element_type x5, other arithmetic, fast_body(): g.astype(F32)  7.64 us

profile of v2, /device:TPU:0, one launch (start us, length us, event | category | flops | bytes accessed | tf_op | source)
XLA Modules:
  0.0 348.7 jit_solution(3586566993733572292)
XLA Ops:
  0.6 1.4 copy.27.refs_4_
  2.0 334.9 %shard_map.220 = (bf16[2,128,768]{2,1,0:T(8,128)(2,1)}, bf16[2,128,768]{2,1,0:T(8,128)(2,1)}, f32[24,768]{1,0:T(8,128)}, bf16[2,96,2304]{2,1,0:T(8,128)(2,1)}, b...) custom-call(bf16[2,128,768]{2,1,0:T(8,128)(2,1)} %refs_0_.1, ...), custom_call_target="tpu_custom_call" | custom-call | tf_op jit(solution)/shard_map/pallas_call | solution.py:1009
  336.9 0.8 constant_dynamic-slice_fusion
  337.7 0.6 fusion
  338.3 0.6 fusion.1
  338.9 0.6 copy.28
  339.5 0.0 copy-start
  339.5 3.0 convert_element_type.17
  342.5 0.0 copy-done
  342.5 0.0 copy-start.1
  342.5 1.6 convert_element_type.19
  344.1 0.0 copy-start.5
  344.1 0.0 copy-done.1
  344.1 0.0 copy-start.4
  344.1 0.0 copy-start.3
  344.1 1.3 convert_element_type.15
  345.4 0.0 copy-done.5
  345.4 0.9 convert_element_type.16
  346.3 0.0 copy-done.4
  346.3 0.9 convert_element_type.18
  347.2 0.0 copy-done.3
  347.2 0.7 copy.31
  347.9 0.0 copy-done.2
  347.9 0.7 copy.32
  (3 shorter events, 0.0 us)
Async XLA Ops:
  339.5 3.0 copy-start
  342.5 1.6 copy-start.1
  344.1 1.3 copy-start.5
  344.1 2.2 copy-start.4
  344.1 3.0 copy-start.3
  345.4 2.5 copy-start.2

commit v3 on v2

--- a/solution.py
+++ b/solution.py
@@ -111,8 +111,10 @@
     def __init__(self, pos, units, shared, send, recv, free, credit, local):
         self.pos, self.units, self.shared = pos, units, shared
         self.send, self.recv, self.free, self.credit, self.local = send, recv, free, credit, local
-        self.turns = 0
+        self.turns = self.emitted = self.cleared = self.paired = self.mark = 0
         self.copies = {}
+        self.steps = self.plan()
+        self.site = 0
 
     def copy(self, u, j, src, dst, device):
         made = remote(src, dst, self.send.at[u, j], self.recv.at[u, j], device)
@@ -120,7 +122,7 @@
         made.start()
 
     def views(self, u):
-        w, landing, out, (r0, rows, c0, cols) = self.units[u]
+        w, landing, out, (r0, rows, c0, cols), _ = self.units[u]
         pos = self.pos
         v = {
             "ar": pl.ds(r0, rows),
@@ -139,28 +141,44 @@
     def emit(self, u):
         w, landing, _, v = self.views(u)
         pos = self.pos
+        assert u == self.emitted
+        self.emitted += 1
         if u >= self.shared:
             pl.semaphore_wait(self.credit.at[u - self.shared], 1)
         self.copy(
             u, 0, w.at[:, 1 - pos.c, v["ar"], v["ac"]], landing.at[:, v["ar"], v["ac"]], pos.partner
         )
 
-    def pair(self, u):
-        w, landing, _, v = self.views(u)
-        pos, c = self.pos, self.pos.c
-        self.copies[u, 0].wait_recv()
-
-        @pl.loop(0, pos.lines)
-        def _(z):
-            w[z, c, v["ar"], v["ac"]] += landing[z, v["ar"], v["ac"]]
-
-        if u < self.shared:
-            signal(self.credit.at[u], pos.partner)
+    def clear(self, u):
+        pos = self.pos
         self.copies[u, 0].wait_send()
         signal(self.free.at[u, 0], pos.first)
         signal(self.free.at[u, 1], pos.second)
         for k in range(1, pos.lines):
             signal(self.free.at[u, 1 + k], pos.along(-k))
+
+    def pair(self, u):
+        w, landing, _, v = self.views(u)
+        pos, c = self.pos, self.pos.c
+        self.copies[u, 0].wait_recv()
+
+        @pl.loop(0, pos.lines)
+        def _(z):
+            w[z, c, v["ar"], v["ac"]] += landing[z, v["ar"], v["ac"]]
+
+        if u < self.shared:
+            signal(self.credit.at[u], pos.partner)
+        if self.units[u][4]:
+            for k in range(1, pos.lines):
+                pl.semaphore_wait(self.free.at[u, 1 + k], 1)
+                self.copy(
+                    u,
+                    2 + k,
+                    w.at[pos.line(k), c, v["ar"], v["ac"]],
+                    w.at[k - 1, 1 - c, v["ar"], v["ac"]],
+                    pos.along(k),
+                )
+            return
         pl.semaphore_wait(self.free.at[u, 0], 1)
         self.copy(u, 1, w.at[:, c, v["ar"], v["fo"]], w.at[:, 1 - c, v["ar"], v["c0"]], pos.first)
 
@@ -204,17 +222,96 @@
         for k in range(1, lines):
             total = total + w[k - 1, 1 - c, v["r1"], v["c1"]].astype(F32)
         w[pos.z, c, v["gh"], v["fh"]] = total.astype(LOW)
+        self.spread(u)
+
+    def spread(self, u):
+        w, _, out, v = self.views(u)
+        pos, c, lines = self.pos, self.pos.c, self.pos.lines
         mine, there = w.at[pos.z, c, v["gh"], v["fh"]], out.at[v["gh"], v["fh"]]
         pltpu.make_async_copy(mine, there, self.local.at[u]).start()
         for j, device in enumerate((pos.first, pos.second, pos.across)):
             self.copy(u, 2 + lines + j, mine, there, device)
 
+    def line_whole(self, u):
+        w, _, _, v = self.views(u)
+        pos, c, lines = self.pos, self.pos.c, self.pos.lines
+        for k in range(1, lines):
+            self.copies[u, 2 + k].wait_recv()
+        total = w[pos.z, c, v["ar"], v["ac"]].astype(F32)
+        for k in range(1, lines):
+            total = total + w[k - 1, 1 - c, v["ar"], v["ac"]].astype(F32)
+        w[pos.z, c, v["ar"], v["ac"]] = total.astype(LOW)
+        pl.semaphore_wait(self.free.at[u, 0], 1)
+        self.copy(
+            u,
+            1,
+            w.at[pos.z, c, v["ar"], v["fo"]],
+            w.at[lines - 1, 1 - c, v["ar"], v["c0"]],
+            pos.first,
+        )
+
+    def one_share(self, u):
+        w, _, _, v = self.views(u)
+        pos, c, lines = self.pos, self.pos.c, self.pos.lines
+        self.copies[u, 1].wait_recv()
+        w[pos.z, c, v["ar"], v["fh"]] += w[lines - 1, 1 - c, v["ar"], v["c0"]]
+        pl.semaphore_wait(self.free.at[u, 1], 1)
+        self.copy(
+            u,
+            2,
+            w.at[pos.z, c, v["go"], v["fh"]],
+            w.at[lines - 1, 1 - c, v["r0"], v["c1"]],
+            pos.second,
+        )
+
+    def two_share(self, u):
+        w, _, _, v = self.views(u)
+        pos, c, lines = self.pos, self.pos.c, self.pos.lines
+        self.copies[u, 2].wait_recv()
+        w[pos.z, c, v["gh"], v["fh"]] += w[lines - 1, 1 - c, v["r0"], v["c1"]]
+        self.spread(u)
+
+    def clears(self, count):
+        while self.cleared < count:
+            self.clear(self.cleared)
+            self.cleared += 1
+
+    def pairs(self, count):
+        self.clears(count)
+        while self.paired < count:
+            self.pair(self.paired)
+            self.paired += 1
+
+    def serve(self, turns):
+        self.pairs(min(self.cleared, self.turns + LEAD))
+        self.clears(self.mark)
+        self.mark = self.emitted
+        for _ in range(turns):
+            if all(u < self.paired for _, u in self.steps.get(self.turns, ())):
+                self.turn()
+
+    def plan(self):
+        plan = {}
+        for u in reversed(range(len(self.units))):
+            whole = self.units[u][4]
+            steps = (self.line_whole, self.one_share, self.two_share) if whole else (self.one, self.two, self.line)
+            lags = (WHOLE_LAG, LAGS[0], LAGS[1]) if whole else LAGS
+            at = u
+            for step, lag in zip(steps, lags):
+                at += lag
+                plan.setdefault(at, []).append((step, u))
+        return plan
+
+    def done(self):
+        return self.turns > max(self.steps)
+
     def turn(self):
-        turn = self.turns
-        self.turns += 1
-        for stage, step in enumerate((self.pair, self.one, self.two, self.line)):
-            if 0 <= turn - stage < len(self.units):
-                step(turn - stage)
+        if not self.done():
+            steps = self.steps.get(self.turns, ())
+            self.turns += 1
+            self.pairs(max([u + 1 for _, u in steps] + [self.paired]))
+            for step, u in steps:
+                step(u)
 
     def finish(self):
         lines = self.pos.lines
@@ -240,6 +337,11 @@
 SAVED_LOW = ("xk", "xv", "xr", "gated", "xk2", "xr2")
 WIDE = 256
 BLOCK = 32
+LEAD = 12
+LINE_FIRST = (2, 5)
+LAGS = (3,3,4)
+WHOLE_LAG = 7
+SITES = (0,)*8+(1,)*24
 VMEM_BYTES = 63 * 2**20
 
 
@@ -299,7 +401,11 @@
             return [(m, (j * (r // count), r // count, 0, c)) for j in range(count)]
         return [(m, (0, r, j * (c // count), c // count)) for j in range(count)]
 
-    layout = pieces(0, 3) + pieces(1, 1) + pieces(2, 3) + pieces(3, 1) + pieces(4, 3)
+    def columns(m, count):
+        _, _, r, c = weights[0][m].shape
+        return [(m, (0, r, j * (c // count), c // count)) for j in range(count)]
+
+    layout = pieces(0, 3) + pieces(1, 1) + pieces(2, 3) + pieces(3, 1) + columns(4, 3)
     per_layer = len(layout)
     gather = Gather(
         pos,
@@ -312,13 +418,14 @@
         gather.begin(u)
 
     kvr = pieces(0, 3)
-    back = pieces(4, 3) + pieces(3, 1) + pieces(2, 3) + pieces(1, 1) + [kvr[2], kvr[0], kvr[1]]
+    back = pieces(3, 1) + pieces(4, 3) + pieces(2, 3) + pieces(1, 1) + [kvr[2], kvr[0], kvr[1]]
+    line_first = LINE_FIRST
     reduce = Reduce(
         pos,
         [
-            (weights[l][m], landing[m], grad_out[m].at[l], box)
+            (weights[l][m], landing[m], grad_out[m].at[l], box, j in line_first)
             for l in reversed(range(layers))
-            for m, box in back
+            for j, (m, box) in enumerate(back)
         ],
         len(back),
         r_send,
@@ -463,7 +570,7 @@
             h = padded[:, span_on(i), :]
             before = padded[:, span(i), :] * spread(live[:, span(i), :])
             for out, j in zip(outs, rates):
-                rate = mix[level, j : j + 1, :]
+                rate = mix[j, level : level + 1, :]
                 out[:, span(i), :] = (h * rate + before * (1.0 - rate)).astype(LOW)
 
     def project(x_ref, w, base, count, put):
@@ -631,10 +738,10 @@
         saved("recept", level)
         project(act["xr2"], w_frec, 0, width, put_in(act["recept"]))
         saving("recept", level)
-        gather.need(base + 10)
         saved("value2", level)
         share = hidden // lines
         for j in range(width // WIDE):
+            gather.need(base + 8 + j)
             total = None
             for z in range(lines):
                 got = dot(
@@ -673,7 +780,7 @@
             direct, shifted = None, None
             for ref, j in zip(d_refs, rates):
                 d = ref[:, span(i), :]
-                rate = mix[level, j : j + 1, :]
+                rate = mix[j, level : level + 1, :]
                 add_vector(level, 2 + j, d * change)
                 direct = d * rate if direct is None else direct + d * rate
                 shifted = d * (1.0 - rate) if shifted is None else shifted + d * (1.0 - rate)
@@ -801,6 +908,10 @@
     ffn_names = ("value2", "recept", "squared", "xk2", "xr2", "x1")
     att_names = tuple(n for n in names if n not in ffn_names)
 
+    def serve():
+        reduce.serve(SITES[reduce.site])
+        reduce.site += 1
+
     def backward_layer(level):
         w_kvr, w_out, w_fkey, w_frec, w_fval = weights[level]
         base = (layers - 1 - level) * per_layer
@@ -816,6 +927,10 @@
             g_low[:, span(i), :] = (g * gate).astype(LOW)
             g_low2[:, span(i), :] = (g * act["value2"][:, span(i), :] * gate * (1.0 - gate)).astype(LOW)
 
+        loaded("xr2", level)
+        back_project(g_low2, w_frec, 0, width, d_two)
+        outer(act["xr2"], g_low2, w_frec, 0, width)
+        reduce.emit(base)
         loaded("squared", level)
 
         @pl.loop(0, lines)
@@ -823,6 +938,8 @@
             got = dot_across(flat(g_low), w_fval[z].reshape(share, width)).reshape(rows, length, share)
             root = jnp.sqrt(act["squared"][:, :, wide(z, 0, share)].astype(F32))
             g_key2[:, :, wide(z, 0, share)] = (got * (2.0 * root)).astype(LOW)
+
+        serve()
 
         @pl.loop(0, lines)
         def _(z):
@@ -833,64 +950,66 @@
                 w_fval[z, :, :, j * WIDE : (j + 1) * WIDE] = got.reshape(2, share // 2, WIDE)
 
         for j in range(3):
-            reduce.emit(base + j)
-        loaded("xr2", level)
-        back_project(g_low2, w_frec, 0, width, d_two)
-        outer(act["xr2"], g_low2, w_frec, 0, width)
-        reduce.emit(base + 3)
-        reduce.turn()
+            reduce.emit(base + 1 + j)
+        serve()
         back_project(g_key2, w_fkey, 0, hidden, d_one)
-        reduce.turn()
+        serve()
         loaded("xk2", level)
         for j in range(3):
             outer(act["xk2"], g_key2, w_fkey, j * third, third, j * third)
             reduce.emit(base + 4 + j)
+            serve()
         loaded("x1", level)
         normalize_into(act["x1"], level, 1)
         blend_back(level, 1, [d_one, d_two], (3, 4))
-        reduce.turn()
+        serve()
 
         def write_att(i, after):
             g_low3[:, span(i), :] = after.astype(LOW)
 
         normalize_back(level, 1, act["x1"], d_one, write_att)
+        serve()
         if level == 1:
             loading(ffn_names)
         back_project(g_low3, w_out, 0, width, main)
         loaded("gated", level)
         outer(act["gated"], g_low3, w_out, 0, width)
         reduce.emit(base + 7)
-        reduce.turn()
+        serve()
         for name in ("logit", "key", "value", "numer", "denom"):
             loaded(name, level)
         after = scan_back_local(level)
+        serve()
         to_low(d_two, g_low)
-        reduce.turn()
         loaded("xr", level)
         back_project(g_low, w_kvr, 2 * width, width, d_three)
         outer(act["xr"], g_low, w_kvr, 2 * width, width)
         reduce.emit(base + 8)
+        serve()
         scan_back_final(level, after)
+        serve()
         to_low(d_one, g_low2)
         to_low(d_two, g_low3)
-        reduce.turn()
         loaded("xk", level)
         loaded("xv", level)
         back_project(g_low2, w_kvr, 0, width, d_one)
         outer(act["xk"], g_low2, w_kvr, 0, width)
         reduce.emit(base + 9)
+        serve()
         back_project(g_low3, w_kvr, width, width, d_two)
         outer(act["xv"], g_low3, w_kvr, width, width)
         reduce.emit(base + 10)
-        reduce.turn()
+        serve()
         loaded("x", level)
         normalize_into(act["x"], level, 0)
         blend_back(level, 0, [d_one, d_two, d_three], (0, 1, 2))
+        serve()
 
         def write_none(i, after):
             g_low[:, span(i), :] = after.astype(LOW)
 
         normalize_back(level, 0, act["x"], d_one, write_none)
+        serve()
         if level == 1:
             loading(att_names)
 
@@ -928,9 +1047,8 @@
 
     for stage in range(5):
         vector_stage(stage)
-        if reduce.turns < len(reduce.units) + 3:
-            reduce.turn()
-    while reduce.turns < len(reduce.units) + 3:
+        reduce.turn()
+    while not reduce.done():
         reduce.turn()
     reduce.finish()
     for j, device in enumerate((pos.partner, pos.first, pos.second)):
@@ -944,6 +1062,51 @@
             edge_sent(2 * layers + index, -1, s > 0)
         for direction in range(2):
             chain_do(level, direction, "wait_send")
+
+
+def finish_kernel(dims, *refs):
+    layers, share, moved = dims
+    ins, sums = refs[:moved], refs[moved]
+    outs = refs[moved + 1 : 2 * moved + 1]
+    decay, first, mix, gain, bias = refs[2 * moved + 1 : 2 * moved + 6]
+    came = refs[2 * moved + 6 : 3 * moved + 6]
+    wide = came[:2] + refs[3 * moved + 6 : 4 * moved + 4]
+    in_sem, out_sem = refs[4 * moved + 4 :]
+    parts = [(i, j) for i in range(moved) for j in range(layers)]
+
+    def arrive(i, j):
+        return pltpu.make_async_copy(ins[i].at[j], came[i].at[j], in_sem.at[i, j])
+
+    def leave(i, j):
+        return pltpu.make_async_copy(wide[i].at[j], outs[i].at[j], out_sem.at[i, j])
+
+    for part in parts:
+        arrive(*part).start()
+    offset = lax.axis_index("dp") * share
+    width = sums.shape[1]
+    own = pltpu.roll(sums[...], lax.rem(width - offset, width), 1)[:, :share]
+    for level in range(layers):
+        at = level * 11
+        decay[level : level + 1, :] = own[at : at + 1]
+        first[level : level + 1, :] = own[at + 1 : at + 2]
+        for j in range(5):
+            mix[j, level : level + 1, :] = own[at + 2 + j : at + 3 + j]
+        for j in range(2):
+            gain[level, j : j + 1, :] = own[at + 7 + j : at + 8 + j]
+            bias[level, j : j + 1, :] = own[at + 9 + j : at + 10 + j]
+    for i, j in parts:
+        arrive(i, j).wait()
+        if i >= 2:
+            rows = ins[i].shape[1]
+
+            @pl.loop(0, rows // 16)
+            def _(k):
+                at = pl.ds(pl.multiple_of(k * 16, 16), 16)
+                wide[i][j, at, :] = came[i][j, at, :].astype(F32)
+
+        leave(i, j).start()
+    for part in parts:
+        leave(*part).wait()
 
 
 def fast_body(
@@ -1015,20 +1178,35 @@
         compiler_params=pltpu.CompilerParams(
             collective_id=0, has_side_effects=True, vmem_limit_bytes=VMEM_BYTES
         ),
-    )(tokens, doc_starts, decay, first, mix, ln_gain, ln_bias, *shards, cotangent)
-    output, grad_tokens, sums = got[:3]
+    )(tokens, doc_starts, decay, first, jnp.swapaxes(mix, 0, 1), ln_gain, ln_bias, *shards, cotangent)
     share = width // lax.axis_size("dp")
-    sums = lax.dynamic_slice_in_dim(sums, lax.axis_index("dp") * share, share, axis=1)
-    sums = sums[: layers * 11].reshape(layers, 11, share)
+    final = [jax.ShapeDtypeStruct(plain, low)] * 2
+    final += [jax.ShapeDtypeStruct(w.shape, F32) for w in shards]
+    final += [jax.ShapeDtypeStruct((layers, share), F32)] * 2
+    final += [jax.ShapeDtypeStruct((5, layers, share), F32)]
+    final += [jax.ShapeDtypeStruct((layers, 2, share), F32)] * 2
+    moved = 2 + len(shards)
+    done = pl.pallas_call(
+        functools.partial(finish_kernel, (layers, share, moved)),
+        out_shape=final,
+        in_specs=[anywhere] * moved + [vmem],
+        out_specs=[anywhere] * moved + [vmem] * 5,
+        scratch_shapes=[pltpu.VMEM(a.shape, low) for a in final[:moved]]
+        + [pltpu.VMEM(a.shape, F32) for a in final[2:moved]]
+        + [dma((moved, layers)), dma((moved, layers))],
+        compiler_params=pltpu.CompilerParams(vmem_limit_bytes=VMEM_BYTES),
+    )(got[0], got[1], *got[3 : 3 + len(shards)], got[2])
+    output, grad_tokens = done[:2]
+    g_decay, g_first, g_mix, g_gain, g_bias = done[moved:]
     return (
         output,
         grad_tokens,
-        sums[:, 0],
-        sums[:, 1],
-        sums[:, 2:7],
-        sums[:, 7:9],
-        sums[:, 9:11],
-        *[g.astype(F32) for g in got[3 : 3 + len(shards)]],
+        g_decay,
+        g_first,
+        jnp.swapaxes(g_mix, 0, 1),
+        g_gain,
+        g_bias,
+        *done[2:moved],
     )
 
 

time: 349 us -> 314 us (0.90)
  Pallas kernels: 335 us -> 313 us
  other arithmetic: 7.64 us -> 0 us
  local copies, waits for them, and re-layouts: 5.48 us -> 0 us
    pallas_call x1, Pallas kernels: 335 us -> 306 us  [fast_body(): pl.pallas_call(functools.partial(train_kernel, (layers, lines, rows, leng...]
    convert_element_type x5 -> x0, other arithmetic: 7.64 us -> none  [fast_body(): g.astype(F32)]
    pallas_call x0 -> x1, Pallas kernels: none -> 6.4 us  [fast_body(): pl.pallas_call(functools.partial(finish_kernel, (layers, share, moved)),...]
    unnamed x16 -> x0, local copies, waits for them, and re-layouts: 3.49 us -> none
where the time goes in v3:
time: 314 us
  Pallas kernels  313 us (100%)
    pallas_call x1, Pallas kernels, fast_body(): pl.pallas_call(functools.partial(train_kernel, (layers, lines, rows, leng...  306 us
    pallas_call x1, Pallas kernels, fast_body(): pl.pallas_call(functools.partial(finish_kernel, (layers, share, moved)),...  6.4 us

profile of v3, /device:TPU:0, one launch (start us, length us, event | category | flops | bytes accessed | tf_op | source)
XLA Modules:
  0.0 313.6 jit_solution(11188222661628822102)
XLA Ops:
  0.6 306.4 %shard_map.220 = (bf16[2,128,768]{2,1,0:T(8,128)(2,1)}, bf16[2,128,768]{2,1,0:T(8,128)(2,1)}, f32[24,768]{1,0:T(8,128)}, bf16[2,96,2304]{2,1,0:T(8,128)(2,1)}, b...) custom-call(bf16[2,128,768]{2,1,0:T(8,128)(2,1)} %refs_0_.1, ...), custom_call_target="tpu_custom_call" | custom-call | tf_op jit(solution)/shard_map/pallas_call | solution.py:1172
  307.0 6.4 %shard_map.221 = (bf16[2,128,768]{2,1,0:T(8,128)(2,1)}, bf16[2,128,768]{2,1,0:T(8,128)(2,1)}, f32[2,96,2304]{2,1,0:T(8,128)}, f32[2,96,768]{2,1,0:T(8,128)}, f32...) custom-call(bf16[2,128,768]{2,1,0:T(8,128)(2,1)} %get-tuple-element., ...), custom_call_target="tpu_custom_call" | custom-call | tf_op jit(solution)/shard_map/pallas_call | solution.py:1189
